TPU v7x, 32 devices: a whole 2x2x4 slice. The times are simulated.
32 devices in a mesh: dp: 16 (over z, y, core), head: 2 (over x).
Axes of the slice: x: 2, y: 2, z: 4, core: 2. Of those that a mesh axis runs over, the one named last changes fastest.
Arguments:
- tokens: bfloat16 [76800, 410], P(('dp', 'head')), may hold values from -6 to 6
- prior_memory: bfloat16 [64, 150, 410], P('dp'), may hold values from -6 to 6
- first_flags: int32 [64], P('dp'), may hold values from 0 to 1
- owners: int32 [7], replicated, may hold values from 0 to 15
- cotangent: float32 [76800, 410], P(('dp', 'head')), may hold values from -6 to 6
- qkvr_master: float32 [4, 410, 410], P(None, None, 'head'), may hold values from -0.3125 to 0.3125
- qkvr_first: float32 [4, 410, 410], P(None, None, 'head'), may hold values from -0.15625 to 0.15625
- qkvr_second: float32 [4, 410, 410], P(None, None, 'head'), may hold values from 5e-05 to 0.0008
- proj_master: float32 [410, 410], P('head'), may hold values from -2.5 to 2.5
- proj_first: float32 [410, 410], P('head'), may hold values from -0.15625 to 0.15625
- proj_second: float32 [410, 410], P('head'), may hold values from 5e-05 to 0.0008
- expand_master: float32 [410, 2100], P(None, 'head'), may hold values from -0.3125 to 0.3125
- expand_first: float32 [410, 2100], P(None, 'head'), may hold values from -0.15625 to 0.15625
- expand_second: float32 [410, 2100], P(None, 'head'), may hold values from 5e-05 to 0.0008
- reduce_master: float32 [2100, 410], P('head'), may hold values from -0.125 to 0.125
- reduce_first: float32 [2100, 410], P('head'), may hold values from -0.15625 to 0.15625
- reduce_second: float32 [2100, 410], P('head'), may hold values from 5e-05 to 0.0008
- headbias_master: float32 [2, 410], P(None, 'head'), may hold values from -3 to 3
- headbias_first: float32 [2, 410], P(None, 'head'), may hold values from -0.15625 to 0.15625
- headbias_second: float32 [2, 410], P(None, 'head'), may hold values from 5e-05 to 0.0008
- expbias_master: float32 [2100], P('head'), may hold values from -3 to 3
- expbias_first: float32 [2100], P('head'), may hold values from -0.15625 to 0.15625
- expbias_second: float32 [2100], P('head'), may hold values from 5e-05 to 0.0008
- norms_master: float32 [5, 410], replicated, may hold values from 0.5 to 1.5
- norms_first: float32 [5, 410], replicated, may hold values from -0.15625 to 0.15625
- norms_second: float32 [5, 410], replicated, may hold values from 5e-05 to 0.0008
Outputs:
- layer_output: float32 [76800, 410], P(('dp', 'head'))
- input_grad: float32 [76800, 410], P(('dp', 'head'))
- group_rms: float32 [7], replicated
- qkvr_grad: float32 [4, 410, 410], P(None, None, 'head')
- qkvr_newfirst: float32 [4, 410, 410], P(None, None, 'head')
- qkvr_newsecond: float32 [4, 410, 410], P(None, None, 'head')
- qkvr_newmaster: float32 [4, 410, 410], P(None, None, 'head')
- proj_grad: float32 [410, 410], P('head')
- proj_newfirst: float32 [410, 410], P('head')
- proj_newsecond: float32 [410, 410], P('head')
- proj_newmaster: float32 [410, 410], P('head')
- expand_grad: float32 [410, 2100], P(None, 'head')
- expand_newfirst: float32 [410, 2100], P(None, 'head')
- expand_newsecond: float32 [410, 2100], P(None, 'head')
- expand_newmaster: float32 [410, 2100], P(None, 'head')
- reduce_grad: float32 [2100, 410], P('head')
- reduce_newfirst: float32 [2100, 410], P('head')
- reduce_newsecond: float32 [2100, 410], P('head')
- reduce_newmaster: float32 [2100, 410], P('head')
- headbias_grad: float32 [2, 410], P(None, 'head')
- headbias_newfirst: float32 [2, 410], P(None, 'head')
- headbias_newsecond: float32 [2, 410], P(None, 'head')
- headbias_newmaster: float32 [2, 410], P(None, 'head')
- expbias_grad: float32 [2100], P('head')
- expbias_newfirst: float32 [2100], P('head')
- expbias_newsecond: float32 [2100], P('head')
- expbias_newmaster: float32 [2100], P('head')
- norms_grad: float32 [5, 410], replicated
- norms_newfirst: float32 [5, 410], replicated
- norms_newsecond: float32 [5, 410], replicated
- norms_newmaster: float32 [5, 410], replicated
- qkvr_copy: bfloat16 [4, 410, 410], P(None, None, 'head')
- proj_copy: bfloat16 [410, 410], P('head')
- expand_copy: bfloat16 [410, 2100], P(None, 'head')
- reduce_copy: bfloat16 [2100, 410], P('head')
Inputs may be any that keep to these rules, and one draw needn't show every extreme that they name: `owners`: several tensors may share an owner.
All inputs are finite; a program needn't handle non-finite values.
Results may differ from a plain program's by a relative error of at most 0.02.
The roundings to bfloat16 on the way count: a program that leaves them out, or rounds other values in their place, can miss the bound.
Values may be sent and summed in bfloat16 or wider, within the bound.
No kernel may reach another device: no remote copies, remote signals or barrier semaphores. Data moves between devices by JAX's collectives and lax.ppermute only.
A program may use at most 384 MiB of HBM per device.

v0:
```python
import math

import jax
import jax.numpy as jnp
from jax import lax
from jax.sharding import PartitionSpec as P

DH = 41
STEP = 10


NORM_EPS = 1e-05
CLIP_LEVEL = 0.01
BETA_ONE = 0.5
BETA_TWO = 0.5
ADAM_EPSILON = 1e-08
WEIGHT_DECAY = 0.1
STEP_RATES = (0.03, 0.2, 0.03, 0.015, 0.3, 0.3, 0.3)
GATE_COEF = 0.7978845608028654


def layer_norm(row_vals, norm_gain, norm_shift):
    center = row_vals - jnp.mean(row_vals, axis=-1, keepdims=True)
    spread = jnp.mean(center * center, axis=-1, keepdims=True)
    return center * lax.rsqrt(spread + NORM_EPS) * norm_gain + norm_shift


def smooth_gate(pre_act):
    return (
        0.5
        * pre_act
        * (1.0 + jnp.tanh(GATE_COEF * (pre_act + 0.044715 * pre_act * pre_act * pre_act)))
    )


def positions(key_len, model_width):
    distance = (key_len - 1 - jnp.arange(key_len)).astype(jnp.float32)
    frequency = jnp.exp(
        jnp.arange(model_width // 2).astype(jnp.float32) * (-2.0 * math.log(10000.0) / model_width)
    )
    angles = distance[:, None] * frequency[None, :]
    return jnp.concatenate([jnp.sin(angles), jnp.cos(angles)], axis=1)


def rel_shift(scores):
    leading = scores.shape[:-2]
    query_len = scores.shape[-2]
    key_len = scores.shape[-1]
    padded = jnp.concatenate([jnp.zeros(leading + (query_len, 1), scores.dtype), scores], axis=-1)
    padded = padded.reshape(leading + (key_len + 1, query_len))
    return padded[..., 1:, :].reshape(scores.shape)


def rel_unshift(shifted):
    leading = shifted.shape[:-2]
    query_len = shifted.shape[-2]
    key_len = shifted.shape[-1]
    flat = shifted.reshape(leading + (query_len * key_len,))
    padded = jnp.concatenate([jnp.zeros(leading + (query_len,), shifted.dtype), flat], axis=-1)
    return padded.reshape(leading + (query_len, key_len + 1))[..., 1:]


def inner_rows(first_op, second_op):
    return lax.dot_general(
        first_op, second_op, (((0,), (0,)), ((), ())), preferred_element_type=jnp.float32
    )


def times_trans(first_op, second_op):
    return lax.dot_general(
        first_op, second_op, (((1,), (1,)), ((), ())), preferred_element_type=jnp.float32
    )


def adam_step(grad_in, first_in, second_in, master_in, clip_factor, step_rate):
    clipped = grad_in * clip_factor
    first_new = BETA_ONE * first_in + (1.0 - BETA_ONE) * clipped
    second_new = BETA_TWO * second_in + (1.0 - BETA_TWO) * clipped * clipped
    first_hat = first_new / (1.0 - BETA_ONE**STEP)
    second_hat = second_new / (1.0 - BETA_TWO**STEP)
    master_new = master_in - step_rate * (
        first_hat / (jnp.sqrt(second_hat) + ADAM_EPSILON) + WEIGHT_DECAY * master_in
    )
    return (clipped, first_new, second_new, master_new)


def clip_factors(squares, counts, owner_ids):
    same = (owner_ids[:, None] == owner_ids[None, :]).astype(jnp.float32)
    mean_sq = jnp.sum(same * squares[None, :], axis=1) / jnp.sum(same * counts[None, :], axis=1)
    return (jnp.sqrt(mean_sq), jnp.minimum(1.0, CLIP_LEVEL * lax.rsqrt(mean_sq + 1e-06)))


def heads_to_rows(head_major):
    n_streams, segs_count, heads_dev, seg_len, head_size = head_major.shape
    return jnp.transpose(head_major, (0, 1, 3, 2, 4)).reshape(
        n_streams * segs_count * seg_len, heads_dev * head_size
    )


def fold_memory(grad_cat, seg_len):
    earlier = grad_cat[:, :, :, :seg_len]
    later = grad_cat[:, :, :, seg_len:]
    own_grad = later + jnp.concatenate([earlier[:, 1:], jnp.zeros_like(earlier[:, :1])], axis=1)
    mem_grad = earlier[:, :1]
    return (
        heads_to_rows(own_grad.astype(jnp.bfloat16)),
        heads_to_rows(mem_grad.astype(jnp.bfloat16)),
    )


def attention_forward(rows_in, prior_flat, flag_vals, qkvr_low, bias_pair, seg_len):
    n_streams = flag_vals.shape[0]
    total_rows, model_width = rows_in.shape
    cols = bias_pair.shape[1]
    heads_dev = cols // DH
    key_len = 2 * seg_len
    segs_count = total_rows // (n_streams * seg_len)
    three = jnp.concatenate([qkvr_low[0], qkvr_low[1], qkvr_low[2]], axis=1)
    pair = jnp.concatenate([qkvr_low[1], qkvr_low[2]], axis=1)
    projected = jnp.dot(rows_in, three, preferred_element_type=jnp.float32).astype(jnp.bfloat16)
    mem_proj = jnp.dot(prior_flat, pair, preferred_element_type=jnp.float32).astype(jnp.bfloat16)
    projected = jnp.transpose(
        projected.reshape(n_streams, segs_count, seg_len, 3, heads_dev, DH), (3, 0, 1, 4, 2, 5)
    )
    mem_proj = jnp.transpose(
        mem_proj.reshape(n_streams, 1, seg_len, 2, heads_dev, DH), (3, 0, 1, 4, 2, 5)
    )
    table = positions(key_len, model_width).astype(jnp.bfloat16)
    rel_keys = jnp.dot(table, qkvr_low[3], preferred_element_type=jnp.float32).astype(jnp.bfloat16)
    rel_heads = jnp.transpose(rel_keys.reshape(key_len, heads_dev, DH), (1, 0, 2))
    rel_wide = jnp.broadcast_to(
        rel_heads[None, None], (n_streams, segs_count, heads_dev, key_len, DH)
    )
    queries, keys, values = (projected[0], projected[1], projected[2])
    mem_keys, mem_values = (mem_proj[0], mem_proj[1])
    key_cat = jnp.concatenate([jnp.concatenate([mem_keys, keys[:, :-1]], axis=1), keys], axis=3)
    value_cat = jnp.concatenate(
        [jnp.concatenate([mem_values, values[:, :-1]], axis=1), values], axis=3
    )
    bias_u = bias_pair[0].reshape(heads_dev, 1, DH)
    bias_v = bias_pair[1].reshape(heads_dev, 1, DH)
    query_float = queries.astype(jnp.float32)
    with_u = (query_float + bias_u).astype(jnp.bfloat16)
    with_v = (query_float + bias_v).astype(jnp.bfloat16)
    content = jnp.einsum("nshid,nshjd->nshij", with_u, key_cat, preferred_element_type=jnp.float32)
    position = rel_shift(
        jnp.einsum("nshid,nshjd->nshij", with_v, rel_wide, preferred_element_type=jnp.float32)
    )
    scale = 1.0 / math.sqrt(DH)
    row_ids = jnp.arange(seg_len)[:, None]
    col_ids = jnp.arange(key_len)[None, :]
    has_memory = (jnp.arange(segs_count)[None, :] > 0) | (flag_vals[:, None] == 1)
    allowed = (col_ids <= row_ids + seg_len) & (
        (col_ids >= seg_len) | has_memory[:, :, None, None, None]
    )
    scores = jnp.where(allowed, (content + position) * scale, -1e30)
    row_peak = jnp.max(scores, axis=-1, keepdims=True)
    expo_vals = jnp.exp(scores - row_peak)
    probs = expo_vals / jnp.sum(expo_vals, axis=-1, keepdims=True)
    probs_low = probs.astype(jnp.bfloat16)
    attended = jnp.einsum(
        "nshij,nshjd->nshid", probs_low, value_cat, preferred_element_type=jnp.float32
    )
    attended = heads_to_rows(attended.astype(jnp.bfloat16))
    saved = (three, table, rel_wide, with_u, with_v, key_cat, value_cat, allowed, probs, probs_low)
    return (attended, saved)


def attention_backward(d_attended_flat, saved, rows_in, prior_flat, seg_len):
    three, table, rel_wide, with_u, with_v, key_cat, value_cat, allowed, probs, probs_low = saved
    n_streams, segs_count, heads_dev, query_len, head_size = with_u.shape
    cols = d_attended_flat.shape[1]
    key_len = 2 * seg_len
    scale = 1.0 / math.sqrt(DH)
    d_attended = jnp.transpose(
        d_attended_flat.reshape(n_streams, segs_count, query_len, heads_dev, head_size),
        (0, 1, 3, 2, 4),
    )
    d_probs = jnp.einsum(
        "nshid,nshjd->nshij", d_attended, value_cat, preferred_element_type=jnp.float32
    )
    d_value_cat = jnp.einsum(
        "nshij,nshid->nshjd", probs_low, d_attended, preferred_element_type=jnp.float32
    )
    d_scores = probs * (d_probs - jnp.sum(d_probs * probs, axis=-1, keepdims=True))
    d_raw = (jnp.where(allowed, d_scores, 0.0) * scale).astype(jnp.bfloat16)
    d_with_u = jnp.einsum("nshij,nshjd->nshid", d_raw, key_cat, preferred_element_type=jnp.float32)
    d_key_cat = jnp.einsum("nshij,nshid->nshjd", d_raw, with_u, preferred_element_type=jnp.float32)
    d_position = rel_unshift(d_raw)
    d_with_v = jnp.einsum(
        "nshic,nshcd->nshid", d_position, rel_wide, preferred_element_type=jnp.float32
    )
    d_rel_heads = jnp.einsum(
        "nshic,nshid->hcd", d_position, with_v, preferred_element_type=jnp.float32
    )
    d_rel_keys = jnp.transpose(d_rel_heads, (1, 0, 2)).reshape(key_len, cols)
    headbias_grad = jnp.stack(
        [
            jnp.sum(d_with_u, axis=(0, 1, 3)).reshape(cols),
            jnp.sum(d_with_v, axis=(0, 1, 3)).reshape(cols),
        ]
    )
    d_queries = heads_to_rows((d_with_u + d_with_v).astype(jnp.bfloat16))
    d_keys, d_mem_keys = fold_memory(d_key_cat, seg_len)
    d_values, d_mem_values = fold_memory(d_value_cat, seg_len)
    d_three = jnp.concatenate([d_queries, d_keys, d_values], axis=1)
    d_pair = jnp.concatenate([d_mem_keys, d_mem_values], axis=1)
    three_grad = inner_rows(rows_in, d_three)
    pair_grad = inner_rows(prior_flat, d_pair)
    rel_grad = inner_rows(table, d_rel_keys.astype(jnp.bfloat16))
    qkvr_grad = jnp.stack(
        [
            three_grad[:, :cols],
            three_grad[:, cols : 2 * cols] + pair_grad[:, :cols],
            three_grad[:, 2 * cols :] + pair_grad[:, cols:],
            rel_grad,
        ]
    )
    return (qkvr_grad, headbias_grad, d_three, three)


def shards(
    tokens,
    prior_memory,
    first_flags,
    owners,
    cotangent,
    qkvr_master,
    qkvr_first,
    qkvr_second,
    proj_master,
    proj_first,
    proj_second,
    expand_master,
    expand_first,
    expand_second,
    reduce_master,
    reduce_first,
    reduce_second,
    headbias_master,
    headbias_first,
    headbias_second,
    expbias_master,
    expbias_first,
    expbias_second,
    norms_master,
    norms_first,
    norms_second,
):
    n_streams, seg_len, model_width = prior_memory.shape
    half_ff = expand_master.shape[1]
    head_pos = lax.axis_index("head")
    heads_count = lax.axis_size("head")
    qkvr_low = qkvr_master.astype(jnp.bfloat16)
    proj_low = proj_master.astype(jnp.bfloat16)
    rows_in, expand_low, reduce_low, expbias_low = (
        lax.all_gather(tokens, "head", axis=0, tiled=True),
        lax.all_gather(expand_master.astype(jnp.bfloat16), "head", axis=1, tiled=True),
        lax.all_gather(reduce_master.astype(jnp.bfloat16), "head", axis=0, tiled=True),
        lax.all_gather(expbias_master.astype(jnp.bfloat16), "head", axis=0, tiled=True),
    )
    prior_flat = prior_memory.reshape(n_streams * seg_len, model_width)
    attended, saved = attention_forward(
        rows_in, prior_flat, first_flags, qkvr_low, headbias_master, seg_len
    )
    attn = lax.psum_scatter(
        jnp.dot(attended, proj_low, preferred_element_type=jnp.float32).astype(jnp.bfloat16),
        "head",
        scatter_dimension=0,
        tiled=True,
    ).astype(jnp.float32)
    resid = tokens.astype(jnp.float32) + attn
    normed, first_norm_back = jax.vjp(layer_norm, resid, norms_master[0], norms_master[1])
    normed_low = normed.astype(jnp.bfloat16)
    pre_act = jnp.dot(
        normed_low, expand_low, preferred_element_type=jnp.float32
    ) + expbias_low.astype(jnp.float32)
    act_float, gate_back = jax.vjp(smooth_gate, pre_act)
    act_low = act_float.astype(jnp.bfloat16)
    second = (
        normed + jnp.dot(act_low, reduce_low, preferred_element_type=jnp.float32) + norms_master[2]
    )
    layer_output, second_norm_back = jax.vjp(layer_norm, second, norms_master[3], norms_master[4])
    d_second, gain_two, shift_two = second_norm_back(cotangent)
    d_second_low = d_second.astype(jnp.bfloat16)
    reduce_grad = inner_rows(act_low, d_second_low)
    (d_pre,) = gate_back(times_trans(d_second_low, reduce_low))
    d_pre_low = d_pre.astype(jnp.bfloat16)
    expand_grad = inner_rows(normed_low, d_pre_low)
    expbias_grad = jnp.sum(d_pre, axis=0)
    d_normed = d_second + times_trans(d_pre_low, expand_low)
    d_resid, gain_one, shift_one = first_norm_back(d_normed)
    norms_grad = jnp.stack([gain_one, shift_one, jnp.sum(d_second, axis=0), gain_two, shift_two])
    attn_back = lax.all_gather(d_resid.astype(jnp.bfloat16), "head", axis=0, tiled=True)
    proj_grad = inner_rows(attended, attn_back)
    d_attended = times_trans(attn_back, proj_low).astype(jnp.bfloat16)
    qkvr_grad, headbias_grad, d_three, three = attention_backward(
        d_attended, saved, rows_in, prior_flat, seg_len
    )
    input_grad = d_resid + lax.psum_scatter(
        times_trans(d_three, three).astype(jnp.bfloat16), "head", scatter_dimension=0, tiled=True
    ).astype(jnp.float32)
    qkvr_grad, proj_grad, headbias_grad = lax.psum((qkvr_grad, proj_grad, headbias_grad), "dp")
    expand_grad, reduce_grad, expbias_grad, norms_grad = lax.psum(
        (expand_grad, reduce_grad, expbias_grad, norms_grad), ("dp", "head")
    )
    expand_grad = lax.dynamic_slice_in_dim(expand_grad, head_pos * half_ff, half_ff, 1)
    reduce_grad = lax.dynamic_slice_in_dim(reduce_grad, head_pos * half_ff, half_ff, 0)
    expbias_grad = lax.dynamic_slice_in_dim(expbias_grad, head_pos * half_ff, half_ff, 0)
    grads = (
        qkvr_grad,
        proj_grad,
        expand_grad,
        reduce_grad,
        headbias_grad,
        expbias_grad,
        norms_grad,
    )
    masters = (
        qkvr_master,
        proj_master,
        expand_master,
        reduce_master,
        headbias_master,
        expbias_master,
        norms_master,
    )
    firsts = (
        qkvr_first,
        proj_first,
        expand_first,
        reduce_first,
        headbias_first,
        expbias_first,
        norms_first,
    )
    seconds = (
        qkvr_second,
        proj_second,
        expand_second,
        reduce_second,
        headbias_second,
        expbias_second,
        norms_second,
    )
    shard_squares = lax.psum(
        jnp.stack([jnp.sum(gradient * gradient) for gradient in grads[:6]]), "head"
    )
    squares = jnp.concatenate([shard_squares, jnp.sum(norms_grad * norms_grad)[None]])
    counts = jnp.array(
        [float(gradient.size * heads_count) for gradient in grads[:6]] + [float(norms_grad.size)],
        jnp.float32,
    )
    group_rms, clips = clip_factors(squares, counts, owners)
    res = [
        adam_step(
            grads[number],
            firsts[number],
            seconds[number],
            masters[number],
            clips[number],
            STEP_RATES[number],
        )
        for number in range(7)
    ]
    return (
        layer_output,
        input_grad,
        group_rms,
        res[0][0],
        res[0][1],
        res[0][2],
        res[0][3],
        res[1][0],
        res[1][1],
        res[1][2],
        res[1][3],
        res[2][0],
        res[2][1],
        res[2][2],
        res[2][3],
        res[3][0],
        res[3][1],
        res[3][2],
        res[3][3],
        res[4][0],
        res[4][1],
        res[4][2],
        res[4][3],
        res[5][0],
        res[5][1],
        res[5][2],
        res[5][3],
        res[6][0],
        res[6][1],
        res[6][2],
        res[6][3],
        res[0][3].astype(jnp.bfloat16),
        res[1][3].astype(jnp.bfloat16),
        res[2][3].astype(jnp.bfloat16),
        res[3][3].astype(jnp.bfloat16),
    )


def solution(mesh):
    in_specs = (
        P(("dp", "head"), None),
        P("dp", None, None),
        P("dp"),
        P(),
        P(("dp", "head"), None),
        P(None, None, "head"),
        P(None, None, "head"),
        P(None, None, "head"),
        P("head", None),
        P("head", None),
        P("head", None),
        P(None, "head"),
        P(None, "head"),
        P(None, "head"),
        P("head", None),
        P("head", None),
        P("head", None),
        P(None, "head"),
        P(None, "head"),
        P(None, "head"),
        P("head"),
        P("head"),
        P("head"),
        P(),
        P(),
        P(),
    )
    out_specs = (
        P(("dp", "head"), None),
        P(("dp", "head"), None),
        P(),
        P(None, None, "head"),
        P(None, None, "head"),
        P(None, None, "head"),
        P(None, None, "head"),
        P("head", None),
        P("head", None),
        P("head", None),
        P("head", None),
        P(None, "head"),
        P(None, "head"),
        P(None, "head"),
        P(None, "head"),
        P("head", None),
        P("head", None),
        P("head", None),
        P("head", None),
        P(None, "head"),
        P(None, "head"),
        P(None, "head"),
        P(None, "head"),
        P("head"),
        P("head"),
        P("head"),
        P("head"),
        P(),
        P(),
        P(),
        P(),
        P(None, None, "head"),
        P("head", None),
        P(None, "head"),
        P("head", None),
    )
    return jax.shard_map(shards, mesh=mesh, in_specs=in_specs, out_specs=out_specs, check_vma=False)
```

profile of v0, /device:TPU:0, one launch (start us, length us, event | category | flops | bytes accessed | tf_op | source)
XLA Modules:
  0.0 1224.0 jit_solution(18033212970947007127)
XLA Ops:
  21.0 46.4 %all-gather.9.cloned.1.call-done = bf16[2,2400,410]{1,2,0:T(8,128)(2,1)} async-done(((bf16[1,2400,410]{1,2,0:T(8,128)(2,1)}), bf16[2,2400,410]{1,2,0:T(8,128)(2,1)}) %all-gather.9.cloned.1.call-update) | async-done | bytes 3936016 | tf_op jit(solution)/shard_map/all_gather | solution.py:257
  67.4 7.2 copy.142
  74.6 9.2 reshape.309
  83.8 8.1 fusion.22
  91.9 31.5 %reshape.285 = bf16[4,8,150,3,5,41]{2,1,0,5,4,3:T(8,128)(2,1)} reshape(bf16[4800,615]{0,1:T(8,128)(2,1)} %fusion.22) | data formatting | bytes 11808000 | tf_op jit(solution)/shard_map/reshape | solution.py:123
  123.4 7.8 copy.209
  140.0 15.7 %fusion.43 = f32[4,8,5,150,300]{4,3,2,1,0:T(8,128)} fusion(f32[5,41]{1,0:T(8,128)S(1)} %add.274, bf16[3,4,8,5,150,41]{4,5,3,2,1,0:T(8,128)(2,1)S(1)} %bitcast.186, bf16[5,300,41]{1,2,0:T(8,128)(2,1)S(1)} %bitcast.191), kind=kOutput, calls=%fused_computation.83 | convolution fusion | flops 593352000 | bytes 32920576 | tf_op jit(solution)/shard_map/nshid,nshjd->nshij/dot_general | solution.py:147
  155.7 29.1 %concatenate.48 = f32[4,8,5,150,301]{4,3,2,1,0:T(8,128)} pad(f32[4,8,5,150,300]{4,3,2,1,0:T(8,128)} %fusion.43, f32[]{:T(128)} %constant.35.clone.1), padding=0_0x0_0x0_0x0_0x1_0 | pad | bytes 57696004 | tf_op jit(solution)/shard_map/concatenate | solution.py:49
  184.8 60.0 %reshape.289 = f32[4,8,5,301,150]{4,3,2,1,0:T(8,128)} reshape(f32[4,8,5,150,301]{4,3,2,1,0:T(8,128)} %concatenate.48) | data formatting | bytes 57792000 | tf_op jit(solution)/shard_map/reshape | solution.py:50
  244.7 33.5 %slice.170 = f32[4,8,5,300,150]{4,3,2,1,0:T(8,128)} slice(f32[4,8,5,301,150]{4,3,2,1,0:T(8,128)} %reshape.289), slice={[0:4], [0:8], [0:5], [1:301], [0:150]} | slice | bytes 57600000 | tf_op jit(solution)/shard_map/slice | solution.py:51
  278.2 48.6 %reshape.290 = f32[4,8,5,150,300]{4,3,2,1,0:T(8,128)} reshape(f32[4,8,5,300,150]{4,3,2,1,0:T(8,128)} %slice.170) | data formatting | bytes 57600000 | tf_op jit(solution)/shard_map/reshape | solution.py:51
  326.8 39.9 %fusion.127 = (f32[4,8,5,150]{3,2,1,0:T(8,128)}, f32[4,8,5,150,300]{4,3,2,1,0:T(8,128)}) fusion(f32[4,8,5,150,300]{4,3,2,1,0:T(8,128)} %reshape.290, pred[4,8,150,300]{3,2,1,0:T(8,128)(4,1)} %broadcast_and_fusion, f32[5,41]{1,0:T(8,128)S(1)} %add.271, bf16[3,4,8,5,150,41]{4,5,3,2,1,0:T(8,128)(2,1)} %bitcast.187, ...), kind=kOutput, calls=%fused_computation.226 | convolution fusion | flops 641160320 | bytes 79916592 | tf_op jit(solution)/shard_map/sub | solution.py:158
  366.7 16.0 %convert_bitcast_fusion = bf16[4,8,150,5,41]{2,4,3,1,0:T(8,128)(2,1)S(1)} fusion(bf16[4,8,5,150,41]{3,4,2,1,0:T(8,128)(2,1)} %copy-done.2, bf16[4,7,5,150,41]{3,4,2,1,0:T(8,128)(2,1)S(1)} %copy-done.11, bf16[4,1,5,150,41]{3,4,2,1,0:T(8,128)(2,1)} %get-tuple-element.239, f32[4,8,5,150,300]{4,3,2,1,0:T(8,128)} %get-tuple-element.258, ...), kind=kOutput, calls=%fused_computation.73 | convolution fusion | flops 617592000 | bytes 34800000 | tf_op jit(solution)/shard_map/nshij,nshjd->nshid/dot_general | solution.py:161
  384.0 8.5 reshape.291
  397.4 7.0 copy.172
  428.7 38.0 %reduce-scatter.7.cloned.1.call-done = bf16[2400,410]{1,0:T(8,128)(2,1)} async-done(((bf16[4800,410]{1,0:T(8,128)(2,1)}), bf16[2400,410]{1,0:T(8,128)(2,1)}) %reduce-scatter.7.cloned.1.call-update) | async-done | bytes 1968016
  474.2 10.2 convolution_add_fusion
  484.4 12.6 %fusion.128 = (f32[2400]{0:T(1024)S(1)}, f32[2400,410]{0,1:T(8,128)S(1)}) fusion(f32[410]{0:T(512)S(1)} %bitcast.208, bf16[2100,410]{0,1:T(8,128)(2,1)S(1)} %copy-done.33, f32[2400,2100]{0,1:T(8,128)} %convolution_add_fusion, f32[410]{0:T(512)S(1)} %bitcast.206, f32[410]{0:T(512)S(1)} %bitcast.197, f32[2400]{0:T(1024)S(1)} %fusion.92, ...), kind=kOutput, calls=%fused_computation.227 | convolution fusion | flops 4187997696 | bytes 29787720 | tf_op jit(solution)/shard_map/dot_general | solution.py:281
  504.9 32.4 %fusion.129 = (f32[2100]{0:T(1024)}, bf16[2400,2100]{0,1:T(8,128)(2,1)}) fusion(f32[2400,2100]{0,1:T(8,128)} %convolution_add_fusion, bf16[2100,410]{0,1:T(8,128)(2,1)S(1)} %copy-done.34, f32[2400,410]{0,1:T(8,128)S(1)} %get-tuple-element.228, f32[2400]{0:T(1024)S(1)} %negate_multiply_fusion.1), kind=kOutput, calls=%fused_computation.228 | convolution fusion | flops 4260768256 | bytes 35916000 | tf_op jit(solution)/shard_map/dot_general | solution.py:70
  537.3 10.2 multiply_reduce_fusion.2
  552.6 13.0 %fusion.23 = f32[410,2100]{1,0:T(8,128)} fusion(bf16[2400,2100]{0,1:T(8,128)(2,1)} %get-tuple-element.263, f32[410]{0:T(512)S(1)} %bitcast.207, f32[410]{0:T(512)S(1)} %bitcast.200, f32[2400]{0:T(1024)S(1)} %fusion.92, f32[2400]{0:T(1024)S(1)} %broadcast_multiply_fusion.4, bf16[2400,410]{0,1:T(8,128)(2,1)} %copy.173, bf16[2400,410]{0,1:T(8,128)(2,1)S(1)} %copy-done.3), kind=kOutput, calls=%fused_computation.47 | convolution fusion | flops 4140672000 | bytes 17482480 | tf_op jit(solution)/shard_map/dot_general | solution.py:64
  565.6 14.1 %fusion.75 = f32[2100,410]{0,1:T(8,128)} fusion(f32[2400,410]{0,1:T(8,128)S(1)} %copy-done.8, f32[2400]{0:T(1024)S(1)} %negate_multiply_fusion.1, f32[2400,2100]{0,1:T(8,128)} %convolution_add_fusion), kind=kOutput, calls=%fused_computation.126 | convolution fusion | flops 4180128000 | bytes 27549600 | tf_op jit(solution)/shard_map/dot_general | solution.py:64
  579.8 28.0 %all-gather.15.cloned.1.call-done = bf16[2,2400,410]{1,2,0:T(8,128)(2,1)} async-done(((bf16[1,2400,410]{1,2,0:T(8,128)(2,1)}), bf16[2,2400,410]{1,2,0:T(8,128)(2,1)}) %all-gather.15.cloned.1.call-update) | async-done | bytes 3936016 | tf_op jit(solution)/shard_map/all_gather | solution.py:294
  607.8 7.1 copy.151
  614.9 9.4 reshape.315
  629.0 10.8 reshape.292
  639.8 15.7 %fusion.14 = f32[4,8,5,300,41]{3,4,2,1,0:T(8,128)S(1)} fusion(bf16[4,8,150,5,41]{2,1,0,4,3:T(8,128)(2,1)S(1)} %reshape.292, f32[4,8,5,150,300]{4,3,2,1,0:T(8,128)} %get-tuple-element.258, f32[4,8,5,150]{3,2,1,0:T(8,128)} %get-tuple-element.257), kind=kOutput, calls=%fused_computation.26 | convolution fusion | flops 604800000 | bytes 38736000 | tf_op jit(solution)/shard_map/nshij,nshid->nshjd/dot_general | solution.py:182
  663.7 18.9 %fusion.35 = f32[4,8,5,150,300]{4,3,2,1,0:T(8,128)} fusion(bf16[4,8,150,5,41]{2,1,0,4,3:T(8,128)(2,1)S(1)} %reshape.292, bf16[4,8,5,150,41]{3,4,2,1,0:T(8,128)(2,1)} %copy-done.2, bf16[4,7,5,150,41]{3,4,2,1,0:T(8,128)(2,1)} %slice.173, bf16[4,1,5,150,41]{3,4,2,1,0:T(8,128)(2,1)} %get-tuple-element.239), kind=kOutput, calls=%fused_computation.71 | convolution fusion | flops 602208000 | bytes 34704000 | tf_op jit(solution)/shard_map/nshid,nshjd->nshij/dot_general | solution.py:179
  682.6 151.6 %multiply_convert_fusion = bf16[4,8,5,150,300]{4,3,2,1,0:T(8,128)(2,1)} fusion(f32[4,8,5,150,300]{4,3,2,1,0:T(8,128)} %fusion.35, pred[4,8,150,300]{3,2,1,0:T(8,128)(4,1)} %broadcast_and_fusion, f32[4,8,5,150,300]{4,3,2,1,0:T(8,128)} %get-tuple-element.258, f32[4,8,5,150]{3,2,1,0:T(8,128)} %get-tuple-element.257), kind=kOutput, calls=%fused_computation.2 | output fusion | flops 57624300 | bytes 73536000 | tf_op jit(solution)/shard_map/sub | solution.py:185
  834.2 12.6 %fusion.45 = f32[4,8,5,300,41]{3,4,2,1,0:T(8,128)} fusion(bf16[4,8,5,150,300]{4,3,2,1,0:T(8,128)(2,1)} %multiply_convert_fusion, f32[5,41]{1,0:T(8,128)S(1)} %copy-done.53, bf16[3,4,8,5,150,41]{4,5,3,2,1,0:T(8,128)(2,1)} %bitcast.188), kind=kOutput, calls=%fused_computation.84 | convolution fusion | flops 593352000 | bytes 30482740 | tf_op jit(solution)/shard_map/nshij,nshid->nshjd/dot_general | solution.py:188
  855.2 13.6 %copy.153 = bf16[4,8,5,150,300]{4,3,1,2,0:T(8,128)(2,1)} copy(bf16[4,8,5,150,300]{4,3,2,1,0:T(8,128)(2,1)} %multiply_convert_fusion) | data formatting | bytes 28800000 | tf_op jit(solution)/shard_map/convert_element_type | solution.py:186
  868.8 23.5 %reshape.293 = bf16[4,8,5,45000]{3,1,2,0:T(8,128)(2,1)} reshape(bf16[4,8,5,150,300]{4,3,1,2,0:T(8,128)(2,1)} %copy.153) | data formatting | bytes 28800000 | tf_op jit(solution)/shard_map/reshape | solution.py:58
  892.4 15.2 %concatenate.51 = bf16[4,8,5,45150]{3,1,2,0:T(8,128)(2,1)} pad(bf16[4,8,5,45000]{3,1,2,0:T(8,128)(2,1)} %reshape.293, bf16[]{:T(256)} %constant.46.clone.1), padding=0_0x0_0x0_0x150_0 | pad | bytes 28848002 | tf_op jit(solution)/shard_map/concatenate | solution.py:59
  907.6 29.6 %reshape.294 = bf16[4,8,5,150,301]{4,3,1,2,0:T(8,128)(2,1)} reshape(bf16[4,8,5,45150]{3,1,2,0:T(8,128)(2,1)} %concatenate.51) | data formatting | bytes 28896000 | tf_op jit(solution)/shard_map/reshape | solution.py:60
  937.2 12.7 %fusion.70 = bf16[300,5,41]{0,2,1:T(8,128)(2,1)} fusion(f32[5,41]{1,0:T(8,128)S(1)} %copy-done.51, bf16[3,4,8,5,150,41]{4,5,3,2,1,0:T(8,128)(2,1)} %bitcast.189, bf16[4,8,5,150,301]{4,3,1,2,0:T(8,128)(2,1)} %reshape.294), kind=kOutput, calls=%fused_computation.119 | convolution fusion | flops 593413504 | bytes 22733740 | tf_op jit(solution)/shard_map/nshic,nshid->hcd/dot_general | solution.py:193
  949.9 13.4 %fusion.12 = f32[4,8,5,150,41]{3,4,2,1,0:T(8,128)} fusion(bf16[5,300,41]{1,2,0:T(8,128)(2,1)S(1)} %bitcast.192, bf16[4,8,5,150,301]{4,3,1,2,0:T(8,128)(2,1)} %reshape.294), kind=kOutput, calls=%fused_computation.21 | convolution fusion | flops 590400000 | bytes 18507000 | tf_op jit(solution)/shard_map/nshic,nshcd->nshid/dot_general | solution.py:190
  964.5 7.2 fusion.33
  973.1 8.5 reshape.297
  983.9 7.4 fusion.32
  992.7 8.5 reshape.296
  1002.2 16.9 %fusion.124 = (f32[5,41]{1,0:T(8,128)S(1)}, bf16[4,8,150,5,41]{2,4,3,1,0:T(8,128)(2,1)}, f32[5,41]{1,0:T(8,128)S(1)}) fusion(f32[4,8,5,150,41]{3,4,2,1,0:T(8,128)} %fusion.12, bf16[4,8,5,150,300]{4,3,2,1,0:T(8,128)(2,1)} %multiply_convert_fusion, bf16[4,8,5,150,41]{3,4,2,1,0:T(8,128)(2,1)} %copy-done.10, bf16[4,7,5,150,41]{3,4,2,1,0:T(8,128)(2,1)} %slice.168, ...), kind=kOutput, calls=%fused_computation.223 | convolution fusion | flops 606143616 | bytes 24241640 | tf_op jit(solution)/shard_map/nshij,nshjd->nshid/dot_general | solution.py:187
  1022.5 8.5 reshape.295
  1034.2 7.3 fusion.58
  1047.2 7.6 convolution_convert_fusion.2
  1054.8 7.1 copy.174
  1065.2 40.0 %all-reduce.5 = (f32[5,410]{1,0:T(8,128)S(1)}, f32[2100]{0:T(1024)S(1)}) all-reduce(f32[5,410]{1,0:T(8,128)S(1)} %stack.63, f32[2100]{0:T(1024)S(1)} %copy-done.62), channel_id=1, replica_groups=mesh['dp'=16,'head'=2] {'dp','head'}, use_global_device_ids=true, to_apply=%region_34.35 | all-reduce | flops 4150 | bytes 33200 | tf_op jit(solution)/shard_map/psum | solution.py:304
  1111.6 32.6 %psum.60 = f32[2,205]{1,0:T(2,128)S(1)} all-reduce(f32[2,205]{1,0:T(2,128)S(1)} %pad_maximum_fusion.18), channel_id=1, replica_groups=mesh['dp'=16,'head'=2] {'dp'}, use_global_device_ids=true, to_apply=%region_23.24 | all-reduce | flops 410 | bytes 3280 | tf_op jit(solution)/shard_map/psum | solution.py:303
  1194.3 15.0 %reduce-scatter.9.cloned.1.call-done = bf16[2400,410]{1,0:T(8,128)(2,1)} async-done(((bf16[4800,410]{1,0:T(8,128)(2,1)}), bf16[2400,410]{1,0:T(8,128)(2,1)}) %reduce-scatter.9.cloned.1.call-update) | async-done | bytes 1968016
  (284 shorter events, 180.3 us)
Async XLA Ops:
  7.2 60.2 %all-gather.9.cloned.1.call-start = ((), (), s32[]{:S(2)}) async-start(), calls=%async_computation.2 | async-start | bytes 6070272 | tf_op jit(solution)/shard_map/all_gather | solution.py:257
  8.0 404.1 %all-gather.11.cloned.1.call-start = ((), (), s32[]{:S(2)}) async-start(), calls=%async_computation.3 | async-start | bytes 2875392 | tf_op jit(solution)/shard_map/all_gather | solution.py:258
  10.7 408.6 %all-gather.13.cloned.1.call-start = ((), (), s32[]{:S(2)}) async-start(), calls=%async_computation.4 | async-start | bytes 2875392 | tf_op jit(solution)/shard_map/all_gather | solution.py:259
  11.8 454.9 %reduce-scatter.7.cloned.1.call-start = ((), (), s32[]{:S(2)}) async-start(), calls=%async_computation.6 | async-start | bytes 7372800
  12.1 314.8 %copy-start.52 = (f32[5,41]{1,0:T(8,128)}, f32[5,41]{1,0:T(8,128)S(1)}, u32[]{:S(2)}) copy-start(f32[5,41]{1,0:T(8,128)S(1)} %add.271) | copy-start | bytes 2464
  12.1 125.2 %copy-start.50 = (f32[5,41]{1,0:T(8,128)}, f32[5,41]{1,0:T(8,128)S(1)}, u32[]{:S(2)}) copy-start(f32[5,41]{1,0:T(8,128)S(1)} %add.274) | copy-start | bytes 2464
  13.5 70.3 %copy-start.42 = (bf16[410,205]{1,0:T(8,128)(2,1)}, bf16[410,205]{1,0:T(8,128)(2,1)S(1)}, u32[]{:S(2)}) copy-start(bf16[410,205]{1,0:T(8,128)(2,1)S(1)} %get-tuple-element.240) | copy-start | bytes 504304
  13.6 70.2 %copy-start.44 = (bf16[410,205]{1,0:T(8,128)(2,1)}, bf16[410,205]{1,0:T(8,128)(2,1)S(1)}, u32[]{:S(2)}) copy-start(bf16[410,205]{1,0:T(8,128)(2,1)S(1)} %get-tuple-element.241) | copy-start | bytes 504304
  13.6 70.2 %copy-start.46 = (bf16[410,205]{1,0:T(8,128)(2,1)}, bf16[410,205]{1,0:T(8,128)(2,1)S(1)}, u32[]{:S(2)}) copy-start(bf16[410,205]{1,0:T(8,128)(2,1)S(1)} %get-tuple-element.242) | copy-start | bytes 504304
  16.1 121.2 %copy-start.18 = (bf16[300,5,41]{0,2,1:T(8,128)(2,1)}, bf16[300,5,41]{0,2,1:T(8,128)(2,1)S(1)}, u32[]{:S(2)}) copy-start(bf16[300,5,41]{0,2,1:T(8,128)(2,1)S(1)} %reshape.288) | copy-start | bytes 369004
  131.2 8.7 copy-start
  326.8 39.9 %copy-start.11 = (bf16[4,7,5,150,41]{3,4,2,1,0:T(8,128)(2,1)S(1)}, bf16[4,7,5,150,41]{3,4,2,1,0:T(8,128)(2,1)}, u32[]{:S(2)}) copy-start(bf16[4,7,5,150,41]{3,4,2,1,0:T(8,128)(2,1)} %slice.173) | copy-start | bytes 5166004
  404.4 7.7 copy-start.56
  404.4 203.3 %all-gather.15.cloned.1.call-start = ((), (), s32[]{:S(2)}) async-start(), calls=%async_computation.5 | async-start | bytes 6070272 | tf_op jit(solution)/shard_map/all_gather | solution.py:294
  423.6 47.5 %copy-start.3 = (bf16[2400,410]{0,1:T(8,128)(2,1)S(1)}, bf16[2400,410]{0,1:T(8,128)(2,1)}, u32[]{:S(2)}) copy-start(bf16[2400,410]{0,1:T(8,128)(2,1)} %param.27) | copy-start | bytes 5904004
  474.2 10.2 copy-start.33
  504.8 32.5 %copy-start.7 = (f32[2400,410]{0,1:T(8,128)}, f32[2400,410]{0,1:T(8,128)S(1)}, u32[]{:S(2)}) copy-start(f32[2400,410]{0,1:T(8,128)S(1)} %get-tuple-element.228) | copy-start | bytes 11808004
  504.8 60.7 %copy-start.54 = (f32[2400]{0:T(1024)}, f32[2400]{0:T(1024)S(1)}, u32[]{:S(2)}) copy-start(f32[2400]{0:T(1024)S(1)} %negate_multiply_fusion.1) | copy-start | bytes 28804
  504.8 32.5 %copy-start.32 = (bf16[2100,410]{0,1:T(8,128)(2,1)S(1)}, bf16[2100,410]{0,1:T(8,128)(2,1)}, u32[]{:S(2)}) copy-start(bf16[2100,410]{0,1:T(8,128)(2,1)} %reshape.311) | copy-start | bytes 5166004
  552.5 553.4 %all-reduce.11.cloned.1.call-start = ((), (), s32[]{:S(2)}) async-start(), calls=%async_computation.8 | async-start | bytes 14483456 | tf_op jit(solution)/shard_map/psum | solution.py:304
  552.6 13.0 %copy-start.8 = (f32[2400,410]{0,1:T(8,128)S(1)}, f32[2400,410]{0,1:T(8,128)}, u32[]{:S(2)}) copy-start(f32[2400,410]{0,1:T(8,128)} %copy-done.7) | copy-start | bytes 11808004
  579.7 565.8 %all-reduce.13.cloned.1.call-start = ((), (), s32[]{:S(2)}) async-start(), calls=%async_computation.9 | async-start | bytes 4259840 | tf_op jit(solution)/shard_map/psum | solution.py:303
  614.9 9.4 copy-start.22
  682.6 151.6 %copy-start.53 = (f32[5,41]{1,0:T(8,128)S(1)}, f32[5,41]{1,0:T(8,128)}, u32[]{:S(2)}) copy-start(f32[5,41]{1,0:T(8,128)} %copy-done.52) | copy-start | bytes 2464
  907.6 29.6 %copy-start.51 = (f32[5,41]{1,0:T(8,128)S(1)}, f32[5,41]{1,0:T(8,128)}, u32[]{:S(2)}) copy-start(f32[5,41]{1,0:T(8,128)} %copy-done.50) | copy-start | bytes 2464
  937.2 12.7 %copy-start.19 = (bf16[300,5,41]{0,2,1:T(8,128)(2,1)S(1)}, bf16[300,5,41]{0,2,1:T(8,128)(2,1)}, u32[]{:S(2)}) copy-start(bf16[300,5,41]{0,2,1:T(8,128)(2,1)} %copy-done.18) | copy-start | bytes 369004
  949.9 13.4 %copy-start.26 = (bf16[4,1,150,5,41]{2,4,3,1,0:T(8,128)(2,1)S(1)}, bf16[4,1,150,5,41]{2,4,3,1,0:T(8,128)(2,1)}, u32[]{:S(2)}) copy-start(bf16[4,1,150,5,41]{2,4,3,1,0:T(8,128)(2,1)} %fusion.80) | copy-start | bytes 738004
  1047.1 162.1 %reduce-scatter.9.cloned.1.call-start = ((), (), s32[]{:S(2)}) async-start(), calls=%async_computation.7 | async-start | bytes 7372800
  1065.1 95.1 %copy-start.71 = (s32[7]{0:T(128)S(1)}, s32[7]{0:T(128)}, u32[]{:S(2)}) copy-start(s32[7]{0:T(128)} %param.30) | copy-start | bytes 88
  1065.1 95.1 %copy-start.74 = (f32[7]{0:T(128)S(1)}, f32[7]{0:T(128)}, u32[]{:S(2)}) copy-start(f32[7]{0:T(128)} %constant.59.clone) | copy-start | bytes 88
  1065.1 96.4 %copy-start.17 = (f32[4,410,205]{2,0,1:T(4,128)S(1)}, f32[4,410,205]{2,0,1:T(4,128)}, u32[]{:S(2)}) copy-start(f32[4,410,205]{2,0,1:T(4,128)} %param.32) | copy-start | bytes 4034404
  1065.1 96.4 %copy-start.36 = (f32[4,410,205]{2,0,1:T(4,128)S(1)}, f32[4,410,205]{2,0,1:T(4,128)}, u32[]{:S(2)}) copy-start(f32[4,410,205]{2,0,1:T(4,128)} %param.34) | copy-start | bytes 4034404
  1169.8 10.9 copy-start.40
  1169.8 10.9 copy-start.41
  1172.0 6.0 copy-start.59
  1172.0 6.0 copy-start.65
  1172.1 5.9 copy-start.66
  1172.1 7.3 copy-start.57
  1172.1 7.3 copy-start.60
  1172.1 7.3 copy-start.61
  1172.1 8.6 copy-start.23
  1172.1 8.5 copy-start.35
  1172.1 10.6 copy-start.27
  1172.1 10.6 copy-start.28
  1174.4 8.3 copy-start.14
  1174.4 8.3 copy-start.21
  1182.7 5.9 copy-start.15
  1194.3 18.1 %copy-start.49 = (f32[2400]{0:T(1024)S(1)}, f32[2400]{0:T(1024)}, u32[]{:S(2)}) copy-start(f32[2400]{0:T(1024)} %copy-done.48) | copy-start | bytes 28804
  (37 other events, 117.9 us)
Sparse Core Ops, SparseCore 0:
  9.6 57.7 all-gather.8
  69.5 31.0 all-gather.10
  102.8 31.0 all-gather.12
  404.6 62.0 reduce-scatter.6
  552.6 55.0 all-gather.14
  613.4 167.2 all-reduce.10
  1047.3 98.1 all-reduce.12
  1147.9 61.3 reduce-scatter.8
where the time goes:
time: 1240 us; the launch traced here: 1220 us
  local copies, waits for them, and re-layouts  473 us (38%)
  matrix products  293 us (24%)
  other arithmetic  229 us (18%)
  waiting for transfers between devices  129 us (10%)
  blocking collectives  83.1 us (7%)
  between operations  16 us (1%)
    sub x1, other arithmetic, attention_backward(): d_probs - jnp.sum(d_probs * probs, axis=-1, keepdims=True)  152 us
    unnamed x172, local copies, waits for them, and re-layouts  75.9 us
    reshape x1, local copies, waits for them, and re-layouts, rel_shift(): padded = padded.reshape(leading + (key_len + 1, query_len))  60 us
    dot_general x4, matrix products, times_trans(): lax.dot_general(first_op, second_op, (((1,), (1,)), ((), ())), preferred_...  55 us
    unnamed x10, waiting for transfers between devices  53.7 us
    reshape x1, local copies, waits for them, and re-layouts, rel_shift(): return padded[..., 1:, :].reshape(scores.shape)  48.6 us
    all_gather x1, waiting for transfers between devices, shards(): lax.all_gather(tokens, 'head', axis=0, tiled=True)  46.4 us
    psum x1, blocking collectives, shards(): lax.psum((expand_grad, reduce_grad, expbias_grad, norms_grad), ('dp', 'he...  40 us
  transfers between devices with their start and end apart: 8, of which 5 were waited for; matrix products, arithmetic and copies ran while one was open for 73% of the time, Pallas kernels for 0%

commit v1 on v0

v1 whole, which is shorter than its diff:
```python
from jax.sharding import PartitionSpec as P
import math
import jax, jax.numpy as jnp
from jax import lax
from jax.experimental import pallas as pl
from jax.experimental.pallas import tpu as pltpu
BF=jnp.bfloat16; F32=jnp.float32
NT=(((1,),(1,)),((),())); TN=(((0,),(0,)),((),()))
def dot(a,b,dn=(((1,),(0,)),((),()))): return lax.dot_general(a,b,dn,preferred_element_type=F32)
SEG=150; NSEG=8; LEN=1200; DH=41; HG=5; CG=205; D=410
RA=96; RQ=160; KA_=256; KB_=384; KC=304
SCALE=1.0/math.sqrt(DH); LOG2E=1.4426950408889634

def fill_rows(x_ref, prior_ref, xs, xcat, xq):
    xs[0:SEG,:]=prior_ref[0].astype(F32)
    xs[SEG:SEG+LEN,:]=x_ref[...].astype(F32)
    xs[SEG+LEN:,:]=jnp.zeros((xs.shape[0]-SEG-LEN,D),F32)
    for s in range(NSEG):
        xcat[s]=xs[SEG*s:SEG*s+KC,:].astype(BF)
        xq[s]=xs[SEG*(s+1):SEG*(s+1)+RQ,:].astype(BF)

def head_masks(rows):
    lane=lax.broadcasted_iota(jnp.int32,(rows,CG),1)
    return [(lane>=DH*h)&(lane<DH*(h+1)) for h in range(HG)]

def ka_kernel(meta, x_ref, prior_ref, wq, wk, wv, relA, relB, bias, att_ref, p_ref, xs, xcat, xq, kbuf, vbuf, attS, biasA, biasB):
    n=pl.program_id(0); s=pl.program_id(1)
    @pl.when(s==0)
    def _():
        fill_rows(x_ref,prior_ref,xs,xcat,xq)
        kbuf[KC:,:]=jnp.zeros((KB_-KC,CG),BF)
        vbuf[KC:,:]=jnp.zeros((KB_-KC,CG),BF)
    has_mem=(s>0)|(meta[1+n]==1)
    jmin=jnp.where(has_mem,0,SEG)
    mem_b=jnp.where(has_mem,0.0,-1e30).astype(F32)
    @pl.when(s<2)
    def _():
        i=lax.broadcasted_iota(jnp.int32,(RA,128),0); j=lax.broadcasted_iota(jnp.int32,(RA,128),1)+128
        biasA[...]=jnp.where((j<=i+SEG)&(j>=jmin),0.0,-1e30)
        i=lax.broadcasted_iota(jnp.int32,(RQ-RA,KB_),0)+RA; j=lax.broadcasted_iota(jnp.int32,(RQ-RA,KB_),1)
        biasB[...]=jnp.where((j<=i+SEG)&(j>=jmin)&(j<2*SEG),0.0,-1e30)
    xc=xcat[s]
    kbuf[0:KC,:]=dot(xc,wk[...]).astype(BF)
    vbuf[0:KC,:]=dot(xc,wv[...]).astype(BF)
    q=dot(xq[s],wq[...]).astype(BF).astype(F32)
    wu=(q+bias[0:1,:]).astype(BF); wvv=(q+bias[1:2,:]).astype(BF)
    hm=head_masks(RQ)
    zero=jnp.zeros((),BF)
    wum=[jnp.where(m,wu,zero) for m in hm]
    wvm=[jnp.where(m,wvv,zero) for m in hm]
    NA=RA; NB=RQ-RA
    SA=dot(jnp.concatenate([w[0:RA] for w in wum],0),kbuf[0:KA_,:],NT)
    PA=dot(jnp.concatenate([w[0:RA] for w in wvm],0),relA[...],NT)
    SB=dot(jnp.concatenate([w[RA:] for w in wum],0),kbuf[...],NT)
    PB=dot(jnp.concatenate([w[RA:] for w in wvm],0),relB[...],NT)
    iA=lax.broadcasted_iota(jnp.int32,(RA,128),0); lA=lax.broadcasted_iota(jnp.int32,(RA,128),1)
    mA=(lA+(105-iA))<128
    iB=lax.broadcasted_iota(jnp.int32,(NB,128),0); lB=lax.broadcasted_iota(jnp.int32,(NB,128),1)
    mB=(lB+(69-iB))<128
    c=SCALE*LOG2E
    pas=[];pbs=[]
    for h in range(HG):
        pa=PA[NA*h:NA*(h+1)]; sa=SA[NA*h:NA*(h+1)]
        r0=pltpu.roll(pa[:,0:128],23,1,stride=1,stride_axis=0)
        r1=pltpu.roll(pa[:,128:256],23,1,stride=1,stride_axis=0)
        t0=(sa[:,0:128]+jnp.where(mA,r0,r1))*c+mem_b
        t1=(sa[:,128:256]+r1)*c+biasA[...]
        mx=jnp.max(jnp.maximum(t0,t1),axis=1,keepdims=True)
        e0=jnp.exp2(t0-mx); e1=jnp.exp2(t1-mx)
        li=1.0/jnp.sum(e0+e1,axis=1,keepdims=True)
        p=jnp.concatenate([(e0*li).astype(BF),(e1*li).astype(BF)],1)
        p_ref[0,0,h,0:RA,0:KA_]=p
        pas.append(p)
        pb=PB[NB*h:NB*(h+1)]; sb=SB[NB*h:NB*(h+1)]
        r0=pltpu.roll(pb[:,0:128],59,1,stride=1,stride_axis=0)
        r1=pltpu.roll(pb[:,128:256],59,1,stride=1,stride_axis=0)
        r2=pltpu.roll(pb[:,256:384],59,1,stride=1,stride_axis=0)
        t0=(sb[:,0:128]+jnp.where(mB,r0,r1))*c+biasB[:,0:128]
        t1=(sb[:,128:256]+jnp.where(mB,r1,r2))*c+biasB[:,128:256]
        t2=(sb[:,256:384]+r2)*c+biasB[:,256:384]
        mx=jnp.max(jnp.maximum(jnp.maximum(t0,t1),t2),axis=1,keepdims=True)
        e0=jnp.exp2(t0-mx); e1=jnp.exp2(t1-mx); e2=jnp.exp2(t2-mx)
        li=1.0/jnp.sum(e0+e1+e2,axis=1,keepdims=True)
        p=jnp.concatenate([(e0*li).astype(BF),(e1*li).astype(BF),(e2*li).astype(BF)],1)
        p_ref[0,0,h,RA:RQ,0:KB_]=p
        pbs.append(p)
    OA=dot(jnp.concatenate(pas,0),vbuf[0:KA_,:])
    OB=dot(jnp.concatenate(pbs,0),vbuf[...])
    hmA=[m[0:RA] for m in hm]; hmB=[m[RA:] for m in hm]
    aA=OA[0:NA]; aB=OB[0:NB]
    for h in range(1,HG):
        aA=jnp.where(hmA[h],OA[NA*h:NA*(h+1)],aA)
        aB=jnp.where(hmB[h],OB[NB*h:NB*(h+1)],aB)
    attS[s,0:RA,:]=aA
    attS[s,RA:RQ,:]=aB
    @pl.when(s==NSEG-1)
    def _():
        for t in range(NSEG):
            xs[SEG*t:SEG*t+152,0:CG]=attS[t,0:152,:]
        att_ref[...]=xs[0:LEN,0:CG].astype(BF)

def attention_fwd(meta,x,prior,wq,wk,wv,relA,relB,bias):
    cst=lambda *sh: pl.BlockSpec(sh,lambda n,s,m: (0,)*len(sh))
    gs=pltpu.PrefetchScalarGridSpec(num_scalar_prefetch=1,grid=(2,NSEG),
      in_specs=[pl.BlockSpec((LEN,D),lambda n,s,m:(n,0)),
        pl.BlockSpec((1,SEG,D),lambda n,s,m:(m[0]*2+n,0,0)),
        cst(D,CG),cst(D,CG),cst(D,CG),cst(KA_,CG),cst(KB_,CG),cst(2,CG)],
      out_specs=[pl.BlockSpec((LEN,CG),lambda n,s,m:(n,0)),
        pl.BlockSpec((1,1,HG,RQ,KB_),lambda n,s,m:(n,s,0,0,0))],
      scratch_shapes=[pltpu.VMEM((1376,D),F32),pltpu.VMEM((NSEG,KC,D),BF),pltpu.VMEM((NSEG,RQ,D),BF),
        pltpu.VMEM((KB_,CG),BF),pltpu.VMEM((KB_,CG),BF),pltpu.VMEM((NSEG,RQ,CG),F32),
        pltpu.VMEM((RA,128),F32),pltpu.VMEM((RQ-RA,KB_),F32)])
    return pl.pallas_call(ka_kernel,grid_spec=gs,name="attn_fwd",
      out_shape=[jax.ShapeDtypeStruct((2*LEN,CG),BF),jax.ShapeDtypeStruct((2,NSEG,HG,RQ,KB_),BF)],
      compiler_params=pltpu.CompilerParams(vmem_limit_bytes=56*2**20))(meta,x,prior,wq,wk,wv,relA,relB,bias)

NORM_EPS = 1e-05
CLIP_LEVEL = 0.01
BETA_ONE = 0.5
BETA_TWO = 0.5
ADAM_EPSILON = 1e-08
WEIGHT_DECAY = 0.1
STEP = 10
STEP_RATES = (0.03, 0.2, 0.03, 0.015, 0.3, 0.3, 0.3)
T=480; HF=1050
G0=0.7978845608028654; G1=0.044715; EPS=1e-5
def ln_fwd(z):
    m=jnp.mean(z,axis=-1,keepdims=True)
    c=z-m
    v=jnp.mean(c*c,axis=-1,keepdims=True)
    r=lax.rsqrt(v+EPS)
    return c*r,r
def ln_bwd(n,r,e):
    return r*(e-jnp.mean(e,axis=-1,keepdims=True)-n*jnp.mean(e*n,axis=-1,keepdims=True))
def kf_kernel(ao,at,x,ct,woo,wot,w1o,w1t,w2o,w2t,b1,nm, lo_ref,dres_ref,g_o,g_t,awo_o,awo_t,aw1_o,aw1_t,aw2_o,aw2_t,gnm_acc):
    i=pl.program_id(0); last=pl.num_programs(0)-1
    @pl.when(i==0)
    def _():
        for r in (awo_o,awo_t,aw1_o,aw1_t,aw2_o,aw2_t,gnm_acc): r[...]=jnp.zeros(r.shape,F32)
    attn=dot(ao[...],woo[...])+dot(at[...],wot[...])
    z=x[...].astype(F32)+attn
    n1,r1=ln_fwd(z)
    normed=n1*nm[0:1]+nm[1:2]
    nl=normed.astype(BF)
    def gate(pre):
        p2=pre*pre
        t=jnp.tanh(G0*pre*(1.0+G1*p2))
        hp=0.5*(1.0+t)
        act=pre*hp
        der=hp+0.5*pre*(1.0-t*t)*(G0*(1.0+3.0*G1*p2))
        return act.astype(BF),der
    acts=[];ders=[]
    second=normed+nm[2:3]
    for k,(w1,w2) in enumerate(((w1o,w2o),(w1t,w2t))):
        pre=dot(nl,w1[...])+b1[k:k+1]
        a,dd=gate(pre)
        acts.append(a);ders.append(dd)
        second=second+dot(a,w2[...])
    n2,r2=ln_fwd(second)
    lo_ref[...]=n2*nm[3:4]+nm[4:5]
    c=ct[...]
    d2=ln_bwd(n2,r2,c*nm[3:4])
    d2l=d2.astype(BF)
    dn=d2
    for k,(w1,w2,aw1,aw2) in enumerate(((w1o,w2o,aw1_o,aw2_o),(w1t,w2t,aw1_t,aw2_t))):
        aw2[0:D]+=dot(d2l,acts[k],TN)
        dpre=dot(d2l,w2[...],NT)*ders[k]
        aw1[D:D+1]+=jnp.sum(dpre,axis=0,keepdims=True)
        dpl=dpre.astype(BF)
        aw1[0:D]+=dot(nl,dpl,TN)
        dn=dn+dot(dpl,w1[...],NT)
    dz=ln_bwd(n1,r1,dn*nm[0:1])
    dres_ref[...]=dz
    dal=dz.astype(BF)
    awo_o[0:CG]+=dot(ao[...],dal,TN)
    awo_t[0:CG]+=dot(at[...],dal,TN)
    gnm=jnp.concatenate([jnp.sum(v,axis=0,keepdims=True) for v in (dn*n1,dn,d2,c*n2,c)],0)
    gnm_acc[0:5]+=gnm
    @pl.when(i==last)
    def _():
        for g,a1,a2,aw in ((g_o,aw1_o,aw2_o,awo_o),(g_t,aw1_t,aw2_t,awo_t)):
            a2[D:D+5,0:D]=gnm_acc[0:5]
            g[0:416]=a1[...].astype(BF)
            g[416:832]=a2[...].astype(BF)
            g[832:960]=jnp.zeros((128,HF),BF)
            g[832:936,0:D]=aw[0:104].astype(BF)
            g[832:936,512:512+D]=aw[104:208].astype(BF)
def ff(ao,at,x,ct,woo,wot,w1o,w1t,w2o,w2t,b1,nm):
    n=x.shape[0]
    row=lambda w: pl.BlockSpec((T,w),lambda i:(i,0))
    cst=lambda *sh: pl.BlockSpec(sh,lambda i:(0,)*len(sh))
    S=jax.ShapeDtypeStruct
    gs=[(960,HF),(960,HF)]
    spec=pl.GridSpec(grid=(n//T,),
      in_specs=[row(CG),row(CG),row(D),row(D),cst(CG,D),cst(CG,D),cst(D,HF),cst(D,HF),cst(HF,D),cst(HF,D),cst(2,HF),cst(5,D)],
      out_specs=[row(D),row(D)]+[cst(*s) for s in gs],
      scratch_shapes=[pltpu.VMEM((208,D),F32)]*2+[pltpu.VMEM((416,HF),F32)]*4+[pltpu.VMEM((8,D),F32)])
    return pl.pallas_call(kf_kernel,name="ff",grid_spec=spec,
      out_shape=[S((n,D),F32),S((n,D),F32)]+[S(s,BF) for s in gs],
      compiler_params=pltpu.CompilerParams(vmem_limit_bytes=60*2**20))(ao,at,x,ct,woo,wot,w1o,w1t,w2o,w2t,b1,nm)
HP=48; GP=HP*HG
def rev8(v):
    idx=7-lax.broadcasted_iota(jnp.int32,v.shape,0)
    return jnp.take_along_axis(v,idx,axis=0)
def unskew(blocks, base, rows):
    nb=len(blocks)
    lane=lax.broadcasted_iota(jnp.int32,(8,128),1); sub=lax.broadcasted_iota(jnp.int32,(8,128),0)
    outs=[[] for _ in blocks]
    for r in range(rows//8):
        sh=base-8*r-7
        rot=[pltpu.roll(rev8(b[8*r:8*r+8]),sh%128,1,stride=1,stride_axis=0) for b in blocks]
        m=lane<(sh+sub)
        for k in range(nb):
            if k==0: o=jnp.where(m,0.0,rot[0])
            else: o=jnp.where(m,rot[k-1],rot[k])
            outs[k].append(rev8(o))
    return [jnp.concatenate(o,0) for o in outs]

def kb_kernel(meta, x_ref, prior_ref, p_ref, dres_ref, base_ref, wq, wk, wv, wo, wqT, wkvT, woT, relA, relB, bias, biasT,
              ig_ref, dwq, dwk, dwv, drA, drB, dbias, xs, xcat, xq, dalS, kbuf, vbuf, ig, draw, dpos, G):
    n=pl.program_id(0); s=pl.program_id(1)
    NA=RA; NB=RQ-RA
    @pl.when((s==0)&(n==0))
    def _():
        for r in (dwq,dwk,dwv,drA,drB,dbias): r[...]=jnp.zeros(r.shape,F32)
        kbuf[KC:,:]=jnp.zeros((KB_-KC,CG),BF)
        vbuf[KC:,:]=jnp.zeros((KB_-KC,CG),BF)
    @pl.when(s==0)
    def _():
        xs[LEN:,:]=jnp.zeros((xs.shape[0]-LEN,D),F32)
        xs[0:LEN,:]=dres_ref[...]
        rows=lax.broadcasted_iota(jnp.int32,(RQ,D),0)
        for t in range(NSEG):
            dalS[t]=jnp.where(rows<SEG,xs[SEG*t:SEG*t+RQ,:],0.0).astype(BF)
        fill_rows(x_ref,prior_ref,xs,xcat,xq)
        xs[SEG:SEG+LEN,:]=base_ref[...]
        for t in range(NSEG+1):
            ig[t]=xs[SEG*t:SEG*t+152,:]
    xc=xcat[s]; xqs=xq[s]; dal=dalS[s]
    kbuf[0:KC,:]=dot(xc,wk[...]).astype(BF)
    vbuf[0:KC,:]=dot(xc,wv[...]).astype(BF)
    qT=dot(wqT[...],xqs,NT).astype(BF).astype(F32)
    wuT=(qT+biasT[:,0:1]).astype(BF); wvT=(qT+biasT[:,1:2]).astype(BF)
    da=dot(dal,wo[...],NT).astype(BF)
    daT=dot(woT[...],dal,NT).astype(BF)
    hm=head_masks(RQ)
    zero=jnp.zeros((),BF)
    dam=[jnp.where(m,da,zero) for m in hm]
    DA=dot(jnp.concatenate([w[0:RA] for w in dam],0),vbuf[0:KA_,:],NT)
    DB=dot(jnp.concatenate([w[RA:] for w in dam],0),vbuf[...],NT)
    dkT=[];dvT=[]
    for h in range(HG):
        pa=p_ref[0,0,h,0:RA,0:KA_]; pb=p_ref[0,0,h,RA:RQ,:]
        pf=pa.astype(F32); dp=DA[NA*h:NA*(h+1)]
        w=dp*pf
        delta=jnp.sum(w[:,0:128]+w[:,128:256],axis=1,keepdims=True)
        dr=(pf*SCALE)*(dp-delta)
        draw[h,0:RA,0:KA_]=dr.astype(BF)
        o=unskew([dr[:,0:128],dr[:,128:256]],105,RA)
        dpos[h,0:RA,0:KA_]=jnp.concatenate([v.astype(BF) for v in o],1)
        pf=pb.astype(F32); dp=DB[NB*h:NB*(h+1)]
        w=dp*pf
        delta=jnp.sum(w[:,0:128]+w[:,128:256]+w[:,256:384],axis=1,keepdims=True)
        dr=(pf*SCALE)*(dp-delta)
        draw[h,RA:RQ,0:KB_]=dr.astype(BF)
        o=unskew([dr[:,0:128],dr[:,128:256],dr[:,256:384]],69,NB)
        dpos[h,RA:RQ,0:KB_]=jnp.concatenate([v.astype(BF) for v in o],1)
        u_=wuT[HP*h:HP*(h+1)]; v_=wvT[HP*h:HP*(h+1)]; d_=daT[HP*h:HP*(h+1)]
        k1=dot(u_,draw[h,:,0:KA_]); k2=dot(u_[:,RA:],draw[h,RA:RQ,KA_:KB_])
        dkT.append(jnp.concatenate([k1,k2],1))
        v1=dot(d_,p_ref[0,0,h,:,0:KA_]); v2=dot(d_[:,RA:],p_ref[0,0,h,RA:RQ,KA_:KB_])
        dvT.append(jnp.concatenate([v1,v2],1))
        drA[HP*h:HP*(h+1)]+=dot(v_[:,0:RA],dpos[h,0:RA,0:KA_])
        drB[HP*h:HP*(h+1)]+=dot(v_[:,RA:],dpos[h,RA:RQ,:])
    def comb(buf,rA,rB):
        OA=dot(jnp.concatenate([buf[h,0:RA,0:KA_] for h in range(HG)],0),rA)
        OB=dot(jnp.concatenate([buf[h,RA:RQ,:] for h in range(HG)],0),rB)
        aA=OA[0:NA]; aB=OB[0:NB]
        for h in range(1,HG):
            aA=jnp.where(hm[h][0:RA],OA[NA*h:NA*(h+1)],aA)
            aB=jnp.where(hm[h][RA:],OB[NB*h:NB*(h+1)],aB)
        return aA,aB
    uA,uB=comb(draw,kbuf[0:KA_,:],kbuf[...])
    vA,vB=comb(dpos,relA[...],relB[...])
    dbias[0:1]+=jnp.sum(uA,0,keepdims=True)+jnp.sum(uB,0,keepdims=True)
    dbias[1:2]+=jnp.sum(vA,0,keepdims=True)+jnp.sum(vB,0,keepdims=True)
    dq=jnp.concatenate([(uA+vA).astype(BF),(uB+vB).astype(BF)],0)
    dk=jnp.concatenate(dkT,0).astype(BF); dv=jnp.concatenate(dvT,0).astype(BF)
    dwq[...]+=dot(dq,xqs,TN)
    dwk[...]+=dot(dk[:,0:KC],xc)
    dwv[...]+=dot(dv[:,0:KC],xc)
    kv=jnp.concatenate([dk[:,0:KC],dv[:,0:KC]],0)
    G[...]=dot(kv,wkvT[...],TN)
    ig[s+1]+=dot(dq,wq[...],NT)[0:152]+G[SEG:SEG+152,:]
    ig[s]+=G[0:152,:]
    @pl.when(s==NSEG-1)
    def _():
        for t in range(NSEG):
            xs[SEG*t:SEG*t+152,:]=ig[t+1]
        ig_ref[...]=xs[0:LEN,:]

def attention_bwd(streams,meta,x,prior,p,dres,base,wq,wk,wv,wo,wqT,wkvT,woT,relA,relB,bias,biasT):
    cst=lambda *sh: pl.BlockSpec(sh,lambda n,s,m: (0,)*len(sh))
    off=streams[0]; ns=len(streams)
    row=lambda w: pl.BlockSpec((LEN,w),lambda n,s,m:(n+off,0))
    own=lambda w: pl.BlockSpec((LEN,w),lambda n,s,m:(n,0))
    S=jax.ShapeDtypeStruct
    gs=pltpu.PrefetchScalarGridSpec(num_scalar_prefetch=1,grid=(ns,NSEG),
      in_specs=[row(D),pl.BlockSpec((1,SEG,D),lambda n,s,m:(m[0]*2+n+off,0,0)),
        pl.BlockSpec((1,1,HG,RQ,KB_),lambda n,s,m:(n+off,s,0,0,0)),row(D),row(D),
        cst(D,CG),cst(D,CG),cst(D,CG),cst(CG,D),cst(GP,D),cst(2*GP,D),cst(GP,D),cst(KA_,CG),cst(KB_,CG),cst(2,CG),cst(GP,2)],
      out_specs=[own(D),cst(CG,D),cst(GP,D),cst(GP,D),cst(GP,KA_),cst(GP,KB_),cst(2,CG)],
      scratch_shapes=[pltpu.VMEM((1376,D),F32),pltpu.VMEM((NSEG,KC,D),BF),pltpu.VMEM((NSEG,RQ,D),BF),pltpu.VMEM((NSEG,RQ,D),BF),
        pltpu.VMEM((KB_,CG),BF),pltpu.VMEM((KB_,CG),BF),pltpu.VMEM((NSEG+1,152,D),F32),
        pltpu.VMEM((HG,RQ,KB_),BF),pltpu.VMEM((HG,RQ,KB_),BF),pltpu.VMEM((KC,D),F32)])
    return pl.pallas_call(kb_kernel,grid_spec=gs,name="attn_bwd",
      out_shape=[S((ns*LEN,D),F32),S((CG,D),F32),S((GP,D),F32),S((GP,D),F32),S((GP,KA_),F32),S((GP,KB_),F32),S((2,CG),F32)],
      compiler_params=pltpu.CompilerParams(vmem_limit_bytes=60*2**20))(meta,x,prior,p,dres,base,wq,wk,wv,wo,wqT,wkvT,woT,relA,relB,bias,biasT)

def pad_heads(wT):
    return jnp.pad(wT.reshape(HG,DH,-1),((0,0),(0,HP-DH),(0,0))).reshape(GP,-1)
def unpad_heads(g):
    return g.reshape(HG,HP,-1)[:,:DH].reshape(CG,-1)
def positions(key_len, model_width):
    distance = (key_len - 1 - jnp.arange(key_len)).astype(jnp.float32)
    frequency = jnp.exp(
        jnp.arange(model_width // 2).astype(jnp.float32) * (-2.0 * math.log(10000.0) / model_width)
    )
    angles = distance[:, None] * frequency[None, :]
    return jnp.concatenate([jnp.sin(angles), jnp.cos(angles)], axis=1)


def adam_step(grad_in, first_in, second_in, master_in, clip_factor, step_rate):
    clipped = grad_in * clip_factor
    first_new = BETA_ONE * first_in + (1.0 - BETA_ONE) * clipped
    second_new = BETA_TWO * second_in + (1.0 - BETA_TWO) * clipped * clipped
    first_hat = first_new / (1.0 - BETA_ONE**STEP)
    second_hat = second_new / (1.0 - BETA_TWO**STEP)
    master_new = master_in - step_rate * (
        first_hat / (jnp.sqrt(second_hat) + ADAM_EPSILON) + WEIGHT_DECAY * master_in
    )
    return (clipped, first_new, second_new, master_new)


def clip_factors(squares, counts, owner_ids):
    same = (owner_ids[:, None] == owner_ids[None, :]).astype(jnp.float32)
    mean_sq = jnp.sum(same * squares[None, :], axis=1) / jnp.sum(same * counts[None, :], axis=1)
    return (jnp.sqrt(mean_sq), jnp.minimum(1.0, CLIP_LEVEL * lax.rsqrt(mean_sq + 1e-06)))


def shards(
    tokens,
    prior_memory,
    first_flags,
    owners,
    cotangent,
    qkvr_master,
    qkvr_first,
    qkvr_second,
    proj_master,
    proj_first,
    proj_second,
    expand_master,
    expand_first,
    expand_second,
    reduce_master,
    reduce_first,
    reduce_second,
    headbias_master,
    headbias_first,
    headbias_second,
    expbias_master,
    expbias_first,
    expbias_second,
    norms_master,
    norms_first,
    norms_second,
):
    heads_count = lax.axis_size("head")
    head = lax.axis_index("head")
    swap = [(h, heads_count - 1 - h) for h in range(heads_count)]
    def other(v):
        return lax.ppermute(v, "head", swap)
    qkvr_own = qkvr_master.astype(BF)
    wo_own = proj_master.astype(BF)
    w1_own = expand_master.astype(BF)
    w2_own = reduce_master.astype(BF)
    b1_own = expbias_master.astype(BF).astype(F32)
    qkvr_oth = other(qkvr_own)
    small = other(jnp.concatenate([headbias_master.reshape(-1), b1_own]))
    wo_oth = other(wo_own)
    w1_oth = other(w1_own)
    w2_oth = other(w2_own)
    hb_oth = small[:2 * CG].reshape(2, CG)
    b1_oth = small[2 * CG:]
    meta = jnp.concatenate([head[None].astype(jnp.int32), lax.dynamic_slice_in_dim(first_flags, head * 2, 2, 0)])
    table = positions(2 * SEG, D).astype(BF)
    def rels(wr):
        rel = jnp.dot(table, wr, preferred_element_type=F32).astype(BF)
        return rel[44:300], jnp.pad(rel, ((16, 68), (0, 0)))
    groups = []
    for w, hb, wo in ((qkvr_own, headbias_master, wo_own), (qkvr_oth, hb_oth, wo_oth)):
        rA, rB = rels(w[3])
        groups.append((w, hb, wo, rA, rB))
    fw = [attention_fwd(meta, tokens, prior_memory, w[0], w[1], w[2], rA, rB, hb) for w, hb, wo, rA, rB in groups]
    layer_output, dres, ff_own, ff_oth = ff(
        fw[0][0], fw[1][0], tokens, cotangent, wo_own, wo_oth, w1_own, w1_oth, w2_own, w2_oth,
        jnp.stack([b1_own, b1_oth]), norms_master)
    n_dp = lax.axis_size("dp")
    dp = lax.axis_index("dp")
    def half_sum(own, oth):
        return own.astype(F32) + other(oth).astype(F32)
    def sum_dp(x):
        n = lax.axis_size("dp")
        me = lax.axis_index("dp")
        b = 1
        while b < n:
            half = x.shape[0] // 2
            up = (me & b) != 0
            send = jnp.where(up, x[:half], x[half:])
            keep = jnp.where(up, x[half:], x[:half])
            got = lax.ppermute(send, "dp", [(i, i ^ b) for i in range(n)])
            x = (keep.astype(F32) + got.astype(F32)).astype(BF)
            b *= 2
        while b > 1:
            b //= 2
            got = lax.ppermute(x, "dp", [(i, i ^ b) for i in range(n)])
            up = (me & b) != 0
            x = jnp.where(up, jnp.concatenate([got, x], 0), jnp.concatenate([x, got], 0))
        return x
    ff_got = other(ff_oth)
    def back(streams, group, p, base):
        w, hb, wo, rA, rB = group
        ph = pad_heads
        ig, dwq, dwk, dwv, drA, drB, db = attention_bwd(streams, meta, tokens, prior_memory, p, dres, base, w[0], w[1], w[2], wo,
            ph(w[0].T), jnp.concatenate([ph(w[1].T), ph(w[2].T)]), ph(wo), rA, rB, hb, ph(hb.T))
        return ig, (dwq, dwk, dwv, drA, drB, db)
    def payload(dwq, dwk, dwv, drA, drB, db):
        dr = unpad_heads(drB[:, 16:316]) + jnp.pad(unpad_heads(drA), ((0, 0), (44, 0)))
        dwr = jnp.dot(dr.astype(BF), table, preferred_element_type=F32)
        return jnp.concatenate([dwq, unpad_heads(dwk), unpad_heads(dwv), dwr, db.reshape(1, D), jnp.zeros((11, D), F32)], 0)
    ig, g_oth = back((0, 1), groups[1], fw[1][1], dres)
    ff_got, g_oth, ig = lax.optimization_barrier((ff_got, g_oth, ig))
    at_got = other(payload(*g_oth).astype(BF))
    chunk = ff_own.shape[0] // n_dp
    half = (ff_own.astype(F32) + ff_got.astype(F32)).astype(BF).reshape(n_dp // 2, 2, chunk, HF)
    odd = (dp & 1) == 1
    send = jnp.where(odd, half[:, 0], half[:, 1])
    keep = jnp.where(odd, half[:, 1], half[:, 0])
    got = lax.ppermute(send, "dp", [(i, i ^ 1) for i in range(n_dp)])
    pair = (keep.astype(F32) + got.astype(F32)).astype(BF)
    pair, ig = lax.optimization_barrier((pair, ig))
    split = lax.all_to_all(pair, "dp", 0, 0, tiled=True, axis_index_groups=[list(range(c, n_dp, 2)) for c in range(2)])
    ig0, g0 = back((0,), groups[0], fw[0][1], ig)
    part = jnp.sum(split.astype(F32), 0).astype(BF)
    part, ig = lax.optimization_barrier((part, ig))
    ff_sum = lax.all_gather(part, "dp", axis=0, tiled=True).astype(F32)
    ig1, g1 = back((1,), groups[0], fw[0][1], ig)
    at_got, ig1, g1 = lax.optimization_barrier((at_got, ig1, g1))
    input_grad = jnp.concatenate([ig0, ig1], 0)
    at_own = payload(*[a + b for a, b in zip(g0, g1)])
    at_half = (at_own + at_got.astype(F32)).astype(BF)
    at_sum = sum_dp(at_half).astype(F32)
    expand_grad = ff_sum[:D]
    expbias_grad = ff_sum[D]
    reduce_grad = ff_sum[416:416 + D].T
    norms_grad = ff_sum[416 + D:416 + D + 5, :D]
    proj_grad = jnp.concatenate([ff_sum[832:936, :D], ff_sum[832:936, 512:512 + D]], 0)[:CG]
    qkvr_grad = jnp.transpose(at_sum[:4 * CG].reshape(4, CG, D), (0, 2, 1))
    headbias_grad = at_sum[4 * CG].reshape(2, CG)
    grads = (
        qkvr_grad,
        proj_grad,
        expand_grad,
        reduce_grad,
        headbias_grad,
        expbias_grad,
        norms_grad,
    )
    masters = (
        qkvr_master,
        proj_master,
        expand_master,
        reduce_master,
        headbias_master,
        expbias_master,
        norms_master,
    )
    firsts = (
        qkvr_first,
        proj_first,
        expand_first,
        reduce_first,
        headbias_first,
        expbias_first,
        norms_first,
    )
    seconds = (
        qkvr_second,
        proj_second,
        expand_second,
        reduce_second,
        headbias_second,
        expbias_second,
        norms_second,
    )
    shard_squares = jnp.stack([jnp.sum(gradient * gradient) for gradient in grads[:6]])
    shard_squares = shard_squares + other(shard_squares)
    squares = jnp.concatenate([shard_squares, jnp.sum(norms_grad * norms_grad)[None]])
    counts = jnp.array(
        [float(gradient.size * heads_count) for gradient in grads[:6]] + [float(norms_grad.size)],
        jnp.float32,
    )
    group_rms, clips = clip_factors(squares, counts, owners)
    res = [
        adam_step(
            grads[number],
            firsts[number],
            seconds[number],
            masters[number],
            clips[number],
            STEP_RATES[number],
        )
        for number in range(7)
    ]
    return (
        layer_output,
        input_grad,
        group_rms,
        res[0][0],
        res[0][1],
        res[0][2],
        res[0][3],
        res[1][0],
        res[1][1],
        res[1][2],
        res[1][3],
        res[2][0],
        res[2][1],
        res[2][2],
        res[2][3],
        res[3][0],
        res[3][1],
        res[3][2],
        res[3][3],
        res[4][0],
        res[4][1],
        res[4][2],
        res[4][3],
        res[5][0],
        res[5][1],
        res[5][2],
        res[5][3],
        res[6][0],
        res[6][1],
        res[6][2],
        res[6][3],
        res[0][3].astype(jnp.bfloat16),
        res[1][3].astype(jnp.bfloat16),
        res[2][3].astype(jnp.bfloat16),
        res[3][3].astype(jnp.bfloat16),
    )


def solution(mesh):
    in_specs = (
        P(("dp", "head"), None),
        P("dp", None, None),
        P("dp"),
        P(),
        P(("dp", "head"), None),
        P(None, None, "head"),
        P(None, None, "head"),
        P(None, None, "head"),
        P("head", None),
        P("head", None),
        P("head", None),
        P(None, "head"),
        P(None, "head"),
        P(None, "head"),
        P("head", None),
        P("head", None),
        P("head", None),
        P(None, "head"),
        P(None, "head"),
        P(None, "head"),
        P("head"),
        P("head"),
        P("head"),
        P(),
        P(),
        P(),
    )
    out_specs = (
        P(("dp", "head"), None),
        P(("dp", "head"), None),
        P(),
        P(None, None, "head"),
        P(None, None, "head"),
        P(None, None, "head"),
        P(None, None, "head"),
        P("head", None),
        P("head", None),
        P("head", None),
        P("head", None),
        P(None, "head"),
        P(None, "head"),
        P(None, "head"),
        P(None, "head"),
        P("head", None),
        P("head", None),
        P("head", None),
        P("head", None),
        P(None, "head"),
        P(None, "head"),
        P(None, "head"),
        P(None, "head"),
        P("head"),
        P("head"),
        P("head"),
        P("head"),
        P(),
        P(),
        P(),
        P(),
        P(None, None, "head"),
        P("head", None),
        P(None, "head"),
        P("head", None),
    )
    return jax.shard_map(shards, mesh=mesh, in_specs=in_specs, out_specs=out_specs, check_vma=False)
```

time: 1240 us -> 496 us (0.40)
  local copies, waits for them, and re-layouts: 473 us -> 84.7 us
  matrix products: 293 us -> 2.12 us
  Pallas kernels: 0 us -> 265 us
  other arithmetic: 229 us -> 60.5 us
  waiting for transfers between devices: 129 us -> 28 us
  blocking collectives: 83.1 us -> 0 us
  starting transfers between devices: 0.33 us -> 30.1 us
    pallas_call x0 -> x6, Pallas kernels: none -> 265 us  [the longest x3 122 us: attention_bwd(): pl.pallas_call(kb_kernel, grid_spec=gs, name='attn_bwd', out_shape=[S((ns...]
    dot_general x24 -> x4, matrix products: 254 us -> 2.12 us  [the longest x2 1.53 us: payload(): dwr = jnp.dot(dr.astype(BF), table, preferred_element_type=F32)]
    reshape x17 -> x23, local copies, waits for them, and re-layouts: 249 us -> 6.2 us  [the longest x1 2.55 us: shards(): (ff_own.astype(F32) + ff_got.astype(F32)).astype(BF)]
    sub x1 -> x0, other arithmetic: 152 us -> none  [attention_backward(): d_probs - jnp.sum(d_probs * probs, axis=-1, keepdims=True)]
    psum x3 -> x0, blocking collectives: 77.7 us -> none  [the longest x1 40 us: shards(): lax.psum((expand_grad, reduce_grad, expbias_grad, norms_grad), ('dp', 'he...]
    all_gather x4 -> x1, waiting for transfers between devices: 74.5 us -> 0.01 us  [shards(): ff_sum = lax.all_gather(part, 'dp', axis=0, tiled=True).astype(F32)]
    unnamed x10 -> x1, waiting for transfers between devices: 53.7 us -> 0.02 us
    unnamed x172 -> x137, local copies, waits for them, and re-layouts: 75.9 us -> 25.6 us
  transfers between devices with their start and end apart: 8 -> 19, of which waited for: 5 -> 8; matrix products, arithmetic and copies ran while one was open for 73% -> 13% of each run, Pallas kernels for 0% -> 43%
where the time goes in v1:
time: 496 us; the launch traced here: 486 us
  Pallas kernels  265 us (53%)
  local copies, waits for them, and re-layouts  84.7 us (17%)
  other arithmetic  60.5 us (12%)
  starting transfers between devices  30.1 us (6%)
  waiting for transfers between devices  28 us (6%)
  between operations  15.6 us (3%)
    pallas_call x3, Pallas kernels, attention_bwd(): pl.pallas_call(kb_kernel, grid_spec=gs, name='attn_bwd', out_shape=[S((ns...  122 us
    pallas_call x2, Pallas kernels, attention_fwd(): pl.pallas_call(ka_kernel, grid_spec=gs, name='attn_fwd', out_shape=[jax.S...  85.7 us
    pallas_call x1, Pallas kernels, ff(): pl.pallas_call(kf_kernel, name='ff', grid_spec=spec, out_shape=[S((n, D),...  58 us
    unnamed x137, local copies, waits for them, and re-layouts  25.6 us
    ppermute x4, waiting for transfers between devices, sum_dp(): got = lax.ppermute(send, 'dp', [(i, i ^ b) for i in range(n)])  14.6 us
    ppermute x8, starting transfers between devices, other(): return lax.ppermute(v, 'head', swap)  12 us
  transfers between devices with their start and end apart: 19, of which 8 were waited for; matrix products, arithmetic and copies ran while one was open for 13% of the time, Pallas kernels for 43%

profile of v1, /device:TPU:0, one launch (start us, length us, event | category | flops | bytes accessed | tf_op | source)
XLA Modules:
  0.0 486.3 jit_solution(5357950119453822386)
XLA Ops:
  7.3 1.8 copy.288
  9.1 1.5 copy.236
  10.7 2.9 collective-permute-start
  13.8 2.1 collective-permute-start.2
  17.1 2.1 collective-permute-start.3
  22.6 2.3 copy.245.w2o
  24.9 4.3 copy.234.x_ref.x
  31.5 5.5 %copy.244.ct = f32[2400,410]{1,0:T(8,128)} copy(f32[2400,410]{0,1:T(8,128)} %param.31) | data formatting | bytes 7872000 | tf_op args[4]
  37.0 42.9 %attn_fwd.2 = (bf16[2400,205]{1,0:T(8,128)(2,1)}, bf16[2,8,5,160,384]{4,3,2,1,0:T(8,128)(2,1)}) custom-call(s32[3]{0:T(128)} %pad_add_fusion.meta, bf16[2400,410]{1,0:T(8,128)(2,1)} %copy.234.x_ref.x, bf16[4,150,410]{2,1,0:T(8,128)(2,1)} %copy.235.prior_ref, bf16[410,205]{1,0:T(8,128)(2,1)} %get-tuple-element.385.wq, ...), custom_call_target="tpu_custom_call" | custom-call | tf_op jit(solution)/shard_map/attn_fwd/pallas_call | solution.py:113
  81.2 4.1 fusion.30
  88.6 42.9 %attn_fwd.3 = (bf16[2400,205]{1,0:T(8,128)(2,1)}, bf16[2,8,5,160,384]{4,3,2,1,0:T(8,128)(2,1)}) custom-call(s32[3]{0:T(128)} %pad_add_fusion.meta, bf16[2400,410]{1,0:T(8,128)(2,1)} %copy.234.x_ref.x, bf16[4,150,410]{2,1,0:T(8,128)(2,1)} %copy.235.prior_ref, bf16[410,205]{1,0:T(8,128)(2,1)} %bitcast.102, bf16[410,205]{1,0:T(8,128)(2,1)} %get-tuple-element.400.wk, ...), custom_call_target="tpu_custom_call" | custom-call | tf_op jit(solution)/shard_map/attn_fwd/pallas_call | solution.py:113
  131.4 2.3 copy.246.w2t
  134.4 58.0 %ff.1 = (f32[2400,410]{1,0:T(8,128)}, f32[2400,410]{1,0:T(8,128)}, bf16[960,1050]{1,0:T(8,128)(2,1)}, bf16[960,1050]{1,0:T(8,128)(2,1)}) custom-call(bf16[2400,205]{1,0:T(8,128)(2,1)} %get-tuple-element.84.ao, bf16[2400,205]{1,0:T(8,128)(2,1)} %get-tuple-element.85.at, bf16[2400,410]{1,0:T(8,128)(2,1)} %copy.234.x_ref.x, f32[2400,410]{1,0:T(8,128)} %copy.244.ct, ...), custom_call_target="tpu_custom_call" | custom-call | tf_op jit(solution)/shard_map/ff/pallas_call | solution.py:198
  192.5 4.2 copy.247
  202.7 58.0 %attn_bwd.3 = (f32[2400,410]{1,0:T(8,128)}, f32[205,410]{1,0:T(8,128)}, f32[240,410]{1,0:T(8,128)}, f32[240,410]{1,0:T(8,128)}, f32[240,256]{1,0:T(8,128)}, /*index=5*/f32[240,384]{1,0:T(8,128)}, f32[2,205]{1,0:T(2,128)}) custom-call(s32[3]{0:T(128)} %pad_add_fusion.meta, bf16[2400,410]{1,0:T(8,128)(2,1)} %copy.234.x_ref.x, ...), custom_call_target="tpu_custom_call" | custom-call | tf_op jit(solution)/shard_map/attn_bwd/pallas_call | solution.py:316
  260.7 3.0 copy.254
  263.6 3.5 add_convert_fusion
  267.2 2.6 reshape.250
  270.6 2.7 collective-permute-done.6
  274.7 6.5 %all-to-all-start = ((bf16[8,60,1050]{2,1,0:T(8,128)(2,1)}), bf16[8,60,1050]{2,1,0:T(8,128)(2,1)S(1)}, u32[]{:S(2)}, u32[]{:S(2)}) async-start(bf16[8,60,1050]{2,1,0:T(8,128)(2,1)} %fusion), calls=%async_computation | async-start | bytes 2359296 | tf_op jit(solution)/shard_map/all_to_all | solution.py:453
  292.6 31.7 %attn_bwd.4 = (f32[1200,410]{1,0:T(8,128)}, f32[205,410]{1,0:T(8,128)}, f32[240,410]{1,0:T(8,128)}, f32[240,410]{1,0:T(8,128)}, f32[240,256]{1,0:T(8,128)}, /*index=5*/f32[240,384]{1,0:T(8,128)}, f32[2,205]{1,0:T(2,128)}) custom-call(s32[3]{0:T(128)} %pad_add_fusion.meta, bf16[2400,410]{1,0:T(8,128)(2,1)} %copy.234.x_ref.x, ...), custom_call_target="tpu_custom_call" | custom-call | tf_op jit(solution)/shard_map/attn_bwd/pallas_call | solution.py:316
  325.3 31.9 %attn_bwd.5 = (f32[1200,410]{1,0:T(8,128)}, f32[205,410]{1,0:T(8,128)}, f32[240,410]{1,0:T(8,128)}, f32[240,410]{1,0:T(8,128)}, f32[240,256]{1,0:T(8,128)}, /*index=5*/f32[240,384]{1,0:T(8,128)}, f32[2,205]{1,0:T(2,128)}) custom-call(s32[3]{0:T(128)} %pad_add_fusion.meta, bf16[2400,410]{1,0:T(8,128)(2,1)} %copy.234.x_ref.x, ...), custom_call_target="tpu_custom_call" | custom-call | tf_op jit(solution)/shard_map/attn_bwd/pallas_call | solution.py:316
  362.3 1.8 copy.266
  366.2 3.0 concatenate.64
  369.6 1.7 collective-permute-done.8
  371.5 2.1 collective-permute-start.9
  373.6 5.5 %collective-permute-done.9 = bf16[208,410]{1,0:T(8,128)(2,1)S(1)} collective-permute-done((bf16[208,410]{1,0:T(8,128)(2,1)S(1)}, bf16[208,410]{1,0:T(8,128)(2,1)S(1)}, u32[]{:S(2)}, u32[]{:S(2)}) %collective-permute-start.9) | collective-permute-done | bytes 170592 | tf_op jit(solution)/shard_map/ppermute | solution.py:422
  379.2 1.8 collective-permute-start.10
  381.0 4.3 collective-permute-done.10
  385.4 3.7 collective-permute-start.11
  389.1 3.1 collective-permute-done.11
  392.3 2.1 collective-permute-start.12
  394.4 3.1 collective-permute-done.12
  397.6 6.0 %collective-permute-done.13 = bf16[104,410]{1,0:T(8,128)(2,1)S(1)} collective-permute-done((bf16[104,410]{1,0:T(8,128)(2,1)S(1)}, bf16[104,410]{1,0:T(8,128)(2,1)S(1)}, u32[]{:S(2)}, u32[]{:S(2)}) %collective-permute-start.13) | collective-permute-done | bytes 85312 | tf_op jit(solution)/shard_map/ppermute | solution.py:427
  403.7 1.7 collective-permute-start.14
  405.3 5.6 %copy.269 = f32[2400,410]{0,1:T(8,128)} copy(f32[2400,410]{1,0:T(8,128)} %get-tuple-element.308) | data formatting | bytes 7872000
  411.2 4.5 pad_maximum_fusion
  415.7 5.4 %copy.270 = f32[2400,410]{0,1:T(8,128)} copy(f32[2400,410]{1,0:T(8,128)} %pad_maximum_fusion) | data formatting | bytes 7872000
  423.0 4.5 reshape.282
  428.7 3.4 multiply_reduce_fusion
  435.5 4.0 stack.39
  439.4 3.4 collective-permute-start.16
  450.3 3.0 copy.271
  453.8 2.0 multiply_subtract_fusion.4
  457.1 8.1 %fusion.17 = (bf16[1050,410]{0,1:T(8,128)(2,1)}, f32[1050,410]{0,1:T(8,128)}, f32[1050,410]{0,1:T(8,128)}, f32[1050,410]{0,1:T(8,128)}, f32[1050,410]{0,1:T(8,128)}) fusion(f32[1050,410]{0,1:T(8,128)S(1)} %copy-done.1, f32[1050,410]{0,1:T(8,128)} %param.43, f32[1050,410]{0,1:T(8,128)} %param.42, f32[]{:T(128)} %bitcast.49, f32[960,1050]{1,0:T(8,128)} %reshape.282), kind=kLoop, calls=%fused_computation.102 | loop fusion | flops 6888000 | bytes 14637004 | tf_op jit(solution)/shard_map/convert_element_type | solution.py:561
  465.3 7.1 %fusion.19 = (bf16[410,1050]{1,0:T(8,128)(2,1)}, f32[410,1050]{1,0:T(8,128)}, f32[410,1050]{1,0:T(8,128)}, f32[410,1050]{1,0:T(8,128)}, f32[410,1050]{1,0:T(8,128)}) fusion(f32[410,1050]{1,0:T(8,128)S(1)} %copy-done.3, f32[410,1050]{1,0:T(8,128)S(1)} %copy-done.12, f32[410,1050]{1,0:T(8,128)S(1)} %copy-done.13, f32[]{:T(128)} %bitcast.48, ...), kind=kLoop, calls=%fused_computation.103 | loop fusion | flops 6888000 | bytes 14637004 | tf_op jit(solution)/shard_map/convert_element_type | solution.py:560
  472.4 2.2 fusion.21
  474.6 4.5 fusion.24
  (270 shorter events, 56.7 us)
Async XLA Ops:
  7.2 6.4 %copy-start.50 = (f32[1050]{0:T(1024)S(1)}, f32[1050]{0:T(1024)}, u32[]{:S(2)}) copy-start(f32[1050]{0:T(1024)} %param.47) | copy-start | bytes 12604
  7.2 6.4 %copy-start.45 = (f32[2,205]{1,0:T(2,128)S(1)}, f32[2,205]{1,0:T(2,128)}, u32[]{:S(2)}) copy-start(f32[2,205]{1,0:T(2,128)} %bias.5) | copy-start | bytes 4924
  7.2 6.5 %copy-start.20 = (f32[205,410]{1,0:T(8,128)S(1)}, f32[205,410]{1,0:T(8,128)}, u32[]{:S(2)}) copy-start(f32[205,410]{1,0:T(8,128)} %param.35) | copy-start | bytes 1008604
  7.2 8.7 %copy-start = (f32[1050,410]{0,1:T(8,128)S(1)}, f32[1050,410]{0,1:T(8,128)}, u32[]{:S(2)}) copy-start(f32[1050,410]{0,1:T(8,128)} %param.41) | copy-start | bytes 5166004
  10.7 70.6 %collective-permute-start = (bf16[4,410,205]{2,0,1:T(4,128)(2,1)}, bf16[4,410,205]{2,0,1:T(4,128)(2,1)}, u32[]{:S(2)}, u32[]{:S(2)}) collective-permute-start(bf16[4,410,205]{2,0,1:T(4,128)(2,1)} %copy.236), channel_id=1, source_target_pairs={{0,1},{1,0},{2,3},{3,2},{4,5},{5,4},{6,7},{7,6},{8,9},{9,8},{10,11... | collective-permute-start | bytes 2017208 | tf_op jit(solution)/shard_map/ppermute | solution.py:383
  13.8 66.1 %collective-permute-start.1 = (f32[1460]{0:T(1024)S(1)}, f32[1460]{0:T(1024)S(1)}, u32[]{:S(2)}, u32[]{:S(2)}) collective-permute-start(f32[1460]{0:T(1024)S(1)} %pad_maximum_fusion.6), channel_id=1, source_target_pairs={{0,1},{1,0},{2,3},{3,2},{4,5},{5,4},{6,7},{7,6},{8,9},{9,8},{10,11... | collective-permute-start | bytes 17528 | tf_op jit(solution)/shard_map/ppermute | solution.py:383
  13.8 119.9 %collective-permute-start.2 = (bf16[205,410]{1,0:T(8,128)(2,1)S(1)}, bf16[205,410]{1,0:T(8,128)(2,1)S(1)}, u32[]{:S(2)}, u32[]{:S(2)}) collective-permute-start(bf16[205,410]{1,0:T(8,128)(2,1)S(1)} %convert_element_type.164.woo.wo), channel_id=1, source_target_pairs={{0,1},{1,0},{2,3},{3,2},{4,5},{5,4},{6,7},{7,6},{8,9},{9,8},{10,11... | collective-permute-start | bytes 504308 | tf_op jit(solution)/shard_map/ppermute | solution.py:383
  16.9 114.5 %collective-permute-start.4 = (bf16[1050,410]{0,1:T(8,128)(2,1)}, bf16[1050,410]{0,1:T(8,128)(2,1)}, u32[]{:S(2)}, u32[]{:S(2)}) collective-permute-start(bf16[1050,410]{0,1:T(8,128)(2,1)} %convert_element_type.166), channel_id=1, source_target_pairs={{0,1},{1,0},{2,3},{3,2},{4,5},{5,4},{6,7},{7,6},{8,9},{9,8},{10,11... | collective-permute-start | bytes 2583008 | tf_op jit(solution)/shard_map/ppermute | solution.py:383
  17.1 7.8 %copy-start.8 = (bf16[410,1050]{1,0:T(8,128)(2,1)}, bf16[410,1050]{1,0:T(8,128)(2,1)S(1)}, u32[]{:S(2)}) copy-start(bf16[410,1050]{1,0:T(8,128)(2,1)S(1)} %convert_element_type.165.w1o) | copy-start | bytes 2583004
  17.1 116.6 %collective-permute-start.3 = (bf16[410,1050]{1,0:T(8,128)(2,1)S(1)}, bf16[410,1050]{1,0:T(8,128)(2,1)}, u32[]{:S(2)}, u32[]{:S(2)}) collective-permute-start(bf16[410,1050]{1,0:T(8,128)(2,1)S(1)} %convert_element_type.165.w1o), channel_id=1, source_target_pairs={{0,1},{1,0},{2,3},{3,2},{4,5},{5,4},{6,7},{7,6},{8,9},{9,8},{10,11... | collective-permute-start | bytes 2583008 | tf_op jit(solution)/shard_map/ppermute | solution.py:383
  20.5 263.5 %copy-start.24 = (bf16[300,205]{1,0:T(8,128)(2,1)}, bf16[300,205]{1,0:T(8,128)(2,1)S(1)}, u32[]{:S(2)}) copy-start(bf16[300,205]{1,0:T(8,128)(2,1)S(1)} %get-tuple-element.390) | copy-start | bytes 369004
  20.5 263.4 %copy-start.26 = (bf16[300,205]{1,0:T(8,128)(2,1)}, bf16[300,205]{1,0:T(8,128)(2,1)S(1)}, u32[]{:S(2)}) copy-start(bf16[300,205]{1,0:T(8,128)(2,1)S(1)} %get-tuple-element.391) | copy-start | bytes 369004
  196.6 64.0 %collective-permute-start.5 = (bf16[960,1050]{0,1:T(8,128)(2,1)}, bf16[960,1050]{0,1:T(8,128)(2,1)}, u32[]{:S(2)}, u32[]{:S(2)}) collective-permute-start(bf16[960,1050]{0,1:T(8,128)(2,1)} %copy.247), channel_id=1, source_target_pairs={{0,1},{1,0},{2,3},{3,2},{4,5},{5,4},{6,7},{7,6},{8,9},{9,8},{10,11... | collective-permute-start | bytes 6048008 | tf_op jit(solution)/shard_map/ppermute | solution.py:383
  270.5 2.8 collective-permute-start.6
  274.7 6.5 %copy-start.41 = (f32[240,384]{1,0:T(8,128)S(1)}, f32[240,384]{1,0:T(8,128)}, u32[]{:S(2)}) copy-start(f32[240,384]{1,0:T(8,128)} %get-tuple-element.106) | copy-start | bytes 1105924
  274.7 6.8 %copy-start.43 = (f32[240,256]{1,0:T(8,128)S(1)}, f32[240,256]{1,0:T(8,128)}, u32[]{:S(2)}) copy-start(f32[240,256]{1,0:T(8,128)} %get-tuple-element.107) | copy-start | bytes 737284
  274.7 49.7 %all-to-all-start = ((bf16[8,60,1050]{2,1,0:T(8,128)(2,1)}), bf16[8,60,1050]{2,1,0:T(8,128)(2,1)S(1)}, u32[]{:S(2)}, u32[]{:S(2)}) async-start(bf16[8,60,1050]{2,1,0:T(8,128)(2,1)} %fusion), calls=%async_computation | async-start | bytes 2359296 | tf_op jit(solution)/shard_map/all_to_all | solution.py:453
  281.2 141.9 %all-gather.3.cloned.1.call-start = ((), (), s32[]{:S(2)}) async-start(), calls=%async_computation.1 | async-start | bytes 2506752 | tf_op jit(solution)/shard_map/all_gather | solution.py:457
  287.1 70.0 %collective-permute-start.7 = (bf16[832,410]{0,1:T(8,128)(2,1)}, bf16[832,410]{0,1:T(8,128)(2,1)}, u32[]{:S(2)}, u32[]{:S(2)}) collective-permute-start(bf16[832,410]{0,1:T(8,128)(2,1)} %copy.263), channel_id=1, source_target_pairs={{0,1},{1,0},{2,3},{3,2},{4,5},{5,4},{6,7},{7,6},{8,9},{9,8},{10,11... | collective-permute-start | bytes 2046728 | tf_op jit(solution)/shard_map/ppermute | solution.py:383
  325.3 31.9 %copy-start.59 = (f32[2,205]{1,0:T(2,128)S(1)}, f32[2,205]{1,0:T(2,128)}, u32[]{:S(2)}) copy-start(f32[2,205]{1,0:T(2,128)} %get-tuple-element.129) | copy-start | bytes 4924
  325.3 32.8 %copy-start.44 = (f32[240,256]{1,0:T(8,128)S(1)}, f32[240,256]{1,0:T(8,128)}, u32[]{:S(2)}) copy-start(f32[240,256]{1,0:T(8,128)} %get-tuple-element.127) | copy-start | bytes 737284
  325.3 33.8 %copy-start.42 = (f32[240,384]{1,0:T(8,128)S(1)}, f32[240,384]{1,0:T(8,128)}, u32[]{:S(2)}) copy-start(f32[240,384]{1,0:T(8,128)} %get-tuple-element.125) | copy-start | bytes 1105924
  369.5 1.8 collective-permute-start.8
  371.5 7.6 %collective-permute-start.9 = (bf16[208,410]{1,0:T(8,128)(2,1)S(1)}, bf16[208,410]{1,0:T(8,128)(2,1)S(1)}, u32[]{:S(2)}, u32[]{:S(2)}) collective-permute-start(bf16[208,410]{1,0:T(8,128)(2,1)S(1)} %broadcast_select_fusion.1), channel_id=1, source_target_pairs={{0,4},{2,6},{4,0},{6,2},{8,12},{10,14},{12,8},{14,10},{16,20},{18,... | collective-permute-start | bytes 511688 | tf_op jit(solution)/shard_map/ppermute | solution.py:422
  379.2 6.1 %collective-permute-start.10 = (bf16[104,410]{1,0:T(8,128)(2,1)S(1)}, bf16[104,410]{1,0:T(8,128)(2,1)S(1)}, u32[]{:S(2)}, u32[]{:S(2)}) collective-permute-start(bf16[104,410]{1,0:T(8,128)(2,1)S(1)} %broadcast_select_fusion.2), channel_id=1, source_target_pairs={{0,8},{2,10},{4,12},{6,14},{8,0},{10,2},{12,4},{14,6},{16,24},{18,... | collective-permute-start | bytes 255848 | tf_op jit(solution)/shard_map/ppermute | solution.py:422
  385.4 6.8 %collective-permute-start.11 = (bf16[52,410]{1,0:T(8,128)(2,1)S(1)}, bf16[52,410]{1,0:T(8,128)(2,1)S(1)}, u32[]{:S(2)}, u32[]{:S(2)}) collective-permute-start(bf16[52,410]{1,0:T(8,128)(2,1)S(1)} %broadcast_select_fusion.3), channel_id=1, source_target_pairs={{0,16},{2,18},{4,20},{6,22},{8,24},{10,26},{12,28},{14,30},{16,0},... | collective-permute-start | bytes 127928 | tf_op jit(solution)/shard_map/ppermute | solution.py:422
  392.3 5.2 %collective-permute-start.12 = (bf16[52,410]{1,0:T(8,128)(2,1)S(1)}, bf16[52,410]{1,0:T(8,128)(2,1)S(1)}, u32[]{:S(2)}, u32[]{:S(2)}) collective-permute-start(bf16[52,410]{1,0:T(8,128)(2,1)S(1)} %add_convert_fusion.9), channel_id=1, source_target_pairs={{0,16},{2,18},{4,20},{6,22},{8,24},{10,26},{12,28},{14,30},{16,0},... | collective-permute-start | bytes 127928 | tf_op jit(solution)/shard_map/ppermute | solution.py:427
  397.5 6.1 %collective-permute-start.13 = (bf16[104,410]{1,0:T(8,128)(2,1)S(1)}, bf16[104,410]{1,0:T(8,128)(2,1)S(1)}, u32[]{:S(2)}, u32[]{:S(2)}) collective-permute-start(bf16[104,410]{1,0:T(8,128)(2,1)S(1)} %maximum_select_fusion.3), channel_id=1, source_target_pairs={{0,8},{2,10},{4,12},{6,14},{8,0},{10,2},{12,4},{14,6},{16,24},{18,... | collective-permute-start | bytes 255848 | tf_op jit(solution)/shard_map/ppermute | solution.py:427
  403.7 7.3 %collective-permute-start.14 = (bf16[208,410]{1,0:T(8,128)(2,1)S(1)}, bf16[208,410]{1,0:T(8,128)(2,1)S(1)}, u32[]{:S(2)}, u32[]{:S(2)}) collective-permute-start(bf16[208,410]{1,0:T(8,128)(2,1)S(1)} %maximum_select_fusion.2), channel_id=1, source_target_pairs={{0,4},{2,6},{4,0},{6,2},{8,12},{10,14},{12,8},{14,10},{16,20},{18,... | collective-permute-start | bytes 511688 | tf_op jit(solution)/shard_map/ppermute | solution.py:427
  411.1 10.0 %collective-permute-start.15 = (bf16[416,410]{1,0:T(8,128)(2,1)S(1)}, bf16[416,410]{1,0:T(8,128)(2,1)S(1)}, u32[]{:S(2)}, u32[]{:S(2)}) collective-permute-start(bf16[416,410]{1,0:T(8,128)(2,1)S(1)} %maximum_select_fusion.1), channel_id=1, source_target_pairs={{0,2},{2,0},{4,6},{6,4},{8,10},{10,8},{12,14},{14,12},{16,18},{18,... | collective-permute-start | bytes 1023368 | tf_op jit(solution)/shard_map/ppermute | solution.py:427
  428.6 16.4 %copy-start.60 = (s32[7]{0:T(128)S(1)}, s32[7]{0:T(128)}, u32[]{:S(2)}) copy-start(s32[7]{0:T(128)} %param.30) | copy-start | bytes 88
  428.7 16.4 %copy-start.62 = (f32[7]{0:T(128)S(1)}, f32[7]{0:T(128)}, u32[]{:S(2)}) copy-start(f32[7]{0:T(128)} %constant.46.clone) | copy-start | bytes 88
  439.4 4.9 %collective-permute-start.16 = (f32[6]{0:T(128)S(1)}, f32[6]{0:T(128)S(1)}, u32[]{:S(2)}, u32[]{:S(2)}) collective-permute-start(f32[6]{0:T(128)S(1)} %stack.39), channel_id=1, source_target_pairs={{0,1},{1,0},{2,3},{3,2},{4,5},{5,4},{6,7},{7,6},{8,9},{9,8},{10,11... | collective-permute-start | bytes 80 | tf_op jit(solution)/shard_map/ppermute | solution.py:383
  447.3 8.6 %copy-start.51 = (f32[1050]{0:T(1024)}, f32[1050]{0:T(1024)S(1)}, u32[]{:S(2)}) copy-start(f32[1050]{0:T(1024)S(1)} %multiply_reduce_fusion.5) | copy-start | bytes 12604
  448.0 8.4 %copy-start.56 = (f32[2,205]{1,0:T(2,128)}, f32[2,205]{1,0:T(2,128)S(1)}, u32[]{:S(2)}) copy-start(f32[2,205]{1,0:T(2,128)S(1)} %mul.374) | copy-start | bytes 4924
  450.3 6.2 %copy-start.47 = (f32[2,205]{1,0:T(2,128)S(1)}, f32[2,205]{1,0:T(2,128)}, u32[]{:S(2)}) copy-start(f32[2,205]{1,0:T(2,128)} %bias.5) | copy-start | bytes 4924
  450.3 6.2 %copy-start.57 = (f32[2,205]{1,0:T(2,128)S(1)}, f32[2,205]{1,0:T(2,128)}, u32[]{:S(2)}) copy-start(f32[2,205]{1,0:T(2,128)} %param.46) | copy-start | bytes 4924
  450.3 6.8 %copy-start.1 = (f32[1050,410]{0,1:T(8,128)S(1)}, f32[1050,410]{0,1:T(8,128)}, u32[]{:S(2)}) copy-start(f32[1050,410]{0,1:T(8,128)} %param.41) | copy-start | bytes 5166004
  457.1 8.1 %copy-start.3 = (f32[410,1050]{1,0:T(8,128)S(1)}, f32[410,1050]{1,0:T(8,128)}, u32[]{:S(2)}) copy-start(f32[410,1050]{1,0:T(8,128)} %param.38) | copy-start | bytes 5166004
  457.1 8.1 %copy-start.12 = (f32[410,1050]{1,0:T(8,128)S(1)}, f32[410,1050]{1,0:T(8,128)}, u32[]{:S(2)}) copy-start(f32[410,1050]{1,0:T(8,128)} %param.40) | copy-start | bytes 5166004
  457.1 8.1 %copy-start.13 = (f32[410,1050]{1,0:T(8,128)S(1)}, f32[410,1050]{1,0:T(8,128)}, u32[]{:S(2)}) copy-start(f32[410,1050]{1,0:T(8,128)} %param.39) | copy-start | bytes 5166004
  465.2 7.2 %copy-start.15 = (f32[104,410]{1,0:T(8,128)S(1)}, f32[104,410]{1,0:T(8,128)}, u32[]{:S(2)}) copy-start(f32[104,410]{1,0:T(8,128)} %copy-done.14) | copy-start | bytes 511684
  465.2 7.2 %copy-start.17 = (f32[104,410]{1,0:T(8,128)S(1)}, f32[104,410]{1,0:T(8,128)}, u32[]{:S(2)}) copy-start(f32[104,410]{1,0:T(8,128)} %copy-done.16) | copy-start | bytes 511684
  465.2 7.2 %copy-start.21 = (f32[205,410]{1,0:T(8,128)S(1)}, f32[205,410]{1,0:T(8,128)}, u32[]{:S(2)}) copy-start(f32[205,410]{1,0:T(8,128)} %param.35) | copy-start | bytes 1008604
  465.2 7.2 %copy-start.39 = (f32[205,410]{1,0:T(8,128)S(1)}, f32[205,410]{1,0:T(8,128)}, u32[]{:S(2)}) copy-start(f32[205,410]{1,0:T(8,128)} %param.37) | copy-start | bytes 1008604
  465.2 7.2 %copy-start.40 = (f32[205,410]{1,0:T(8,128)S(1)}, f32[205,410]{1,0:T(8,128)}, u32[]{:S(2)}) copy-start(f32[205,410]{1,0:T(8,128)} %param.36) | copy-start | bytes 1008604
  465.3 9.3 %copy-start.22 = (f32[4,410,205]{2,0,1:T(4,128)S(1)}, f32[4,410,205]{2,0,1:T(4,128)}, u32[]{:S(2)}) copy-start(f32[4,410,205]{2,0,1:T(4,128)} %param.34) | copy-start | bytes 4034404
  465.3 9.3 %copy-start.23 = (f32[4,410,205]{2,0,1:T(4,128)S(1)}, f32[4,410,205]{2,0,1:T(4,128)}, u32[]{:S(2)}) copy-start(f32[4,410,205]{2,0,1:T(4,128)} %param.33) | copy-start | bytes 4034404
  (35 other events, 127.2 us)
Sparse Core Ops, SparseCore 0:
  369.7 46.3 all-gather.2
